TPU v7x, 128 devices: a whole 4x4x4 slice. The times are simulated.
128 devices in a mesh: shot: 8 (over x, core), rline: 16 (over y, z).
Axes of the slice: x: 4, y: 4, z: 4, core: 2. Of those that a mesh axis runs over, the one named last changes fastest.
Arguments:
- shot_traces: bfloat16 [8, 288, 128, 2048], P('shot', 'rline'), may hold values from -6 to 6
- slot_dest: int32 [8, 288], P('shot', 'rline'), may hold values from 0 to 15, as said below
- slot_offset: int32 [8, 288], P('shot', 'rline'), may hold values from 0 to 8, as said below
- block_count: int32 [8, 16], P('shot', 'rline'), may hold values from 0 to 18, as said below
- amp_index: int32 [8, 288, 128], P('shot', 'rline'), may hold values from 0 to 1023
- amp_table: float32 [1024], P('shot'), may hold values from 0.1 to 0.6
- dip_trace: bfloat16 [8, 32], replicated, may hold values from -1 to 1
- dip_time: bfloat16 [8, 64], replicated, may hold values from -0.25 to 0.25
Outputs:
- filtered: bfloat16 [8, 288, 128, 2048], P('shot', 'rline')
Inputs may be any that keep to these rules, and one draw needn't show every extreme that they name: Within each shot row, every pair (slot_dest, slot_offset) is named by exactly one live slot; a device's live slots name one destination at most 2 times, and some device names one destination exactly 2 times. The devices at rline indices 2m and 2m + 1 together hold 18 live slots; of the one holding more (either when equal), the first 9 slots name one destination at most 1 times, and so do its live slots from 9 on together with the other device's live slots; some such set names one destination exactly 1 times. Dead slots hold 0. `slot_offset`: dead slots hold 0. `block_count`: each shot row's counts sum to 144, and those of rline indices 2m and 2m + 1 to 18; in every row some device holds exactly 18 live slots and some holds none.
All inputs are finite; a program needn't handle non-finite values.
Results may differ from a plain program's by a relative error of at most 0.0034.
Values may be sent and summed in bfloat16 or wider, within the bound.
No kernel may reach another device: no remote copies, remote signals or barrier semaphores. Data moves between devices by JAX's collectives and lax.ppermute only.
A program may use at most 128 MiB of HBM per device.

v0:
```python
import jax
import jax.numpy as jnp
from jax import lax
from jax.sharding import PartitionSpec as P

tile_len = 128


def extended_2(array, sides, width):
    for axis, dim in sides:
        devices, length = (lax.axis_size(axis), array.shape[dim])
        up = [(i, (i + 1) % devices) for i in range(devices - 1)]
        down = [(j, i) for i, j in up]
        last = lax.slice_in_dim(array, length - width, length, axis=dim)
        first = lax.slice_in_dim(array, 0, width, axis=dim)
        before = lax.ppermute(last, axis, up)
        after = lax.ppermute(first, axis, down)
        array = jnp.concatenate([before, array, after], axis=dim)
    return array


def band_matrix(tap_values, out_len, in_len, shift):
    tap_total = tap_values.shape[1]
    row_grid = lax.broadcasted_iota(jnp.int32, (out_len, in_len), 0)
    col_grid = lax.broadcasted_iota(jnp.int32, (out_len, in_len), 1)
    tap_index = col_grid + shift - row_grid
    onehot = (
        tap_index[None, :, :] == jnp.arange(tap_total, dtype=jnp.int32)[:, None, None]
    ).astype(jnp.float32)
    return jnp.einsum(
        "ck,kiu->ciu", tap_values.astype(jnp.float32), onehot, precision=lax.Precision.HIGHEST
    ).astype(jnp.bfloat16)


def filter_block(padded, weights, block_idx, matrices):
    trace_main, trace_tail, time_main, time_tail = matrices
    dip_total = trace_main.shape[0]
    block_len = trace_main.shape[1]
    taps_x = trace_tail.shape[2]
    taps_t = time_tail.shape[2]
    sample_total = padded.shape[1]
    window = lax.dynamic_slice_in_dim(padded, block_idx * block_len, block_len + taps_x, 0)
    trace_pass = jnp.einsum(
        "ciu,ut->cit", trace_main, window[:block_len], preferred_element_type=jnp.float32
    )
    trace_pass = trace_pass + jnp.einsum(
        "ciu,ut->cit", trace_tail, window[block_len:], preferred_element_type=jnp.float32
    )
    trace_pass = trace_pass.astype(jnp.bfloat16)
    time_padded = jnp.pad(trace_pass, ((0, 0), (0, 0), (taps_t // 2, tile_len - taps_t // 2)))
    time_padded = time_padded.reshape(dip_total, block_len, sample_total // tile_len + 1, tile_len)
    time_pass = jnp.einsum(
        "crbu,ciu->rbi", time_padded[:, :, :-1], time_main, preferred_element_type=jnp.float32
    )
    time_pass = time_pass + jnp.einsum(
        "crbu,ciu->rbi",
        time_padded[:, :, 1:, :taps_t],
        time_tail,
        preferred_element_type=jnp.float32,
    )
    weight = lax.dynamic_slice_in_dim(weights, block_idx * block_len, block_len, 0)
    center = window[taps_x // 2 : taps_x // 2 + block_len].astype(jnp.float32)
    return (center - weight[:, None] * time_pass.reshape(block_len, sample_total)).astype(
        jnp.bfloat16
    )


def pack_blocks(traces, index_rows, destination, position, live_mask, capacity, line_count):
    slot_total = traces.shape[0]
    rows_out = line_count * capacity
    slot_ids = jnp.arange(slot_total, dtype=jnp.int32)
    earlier = (
        (destination[None, :] == destination[:, None])
        & live_mask[None, :]
        & (slot_ids[None, :] < slot_ids[:, None])
    )
    slot_rank = jnp.sum(earlier.astype(jnp.int32), axis=1)
    buffer_row = jnp.where(live_mask, destination * capacity + slot_rank, rows_out)
    buffer_hit = buffer_row[None, :] == jnp.arange(rows_out, dtype=jnp.int32)[:, None]
    source_slot = jnp.sum(jnp.where(buffer_hit, slot_ids[None, :], 0), axis=1)
    filled = jnp.any(buffer_hit, axis=1)
    outgoing = jnp.where(
        filled[:, None, None], jnp.take(traces, source_slot, axis=0), jnp.zeros((), jnp.bfloat16)
    )
    outgoing_index = jnp.where(filled[:, None], jnp.take(index_rows, source_slot, axis=0), 0)
    outgoing_tag = jnp.where(filled, jnp.take(position, source_slot, axis=0) + 1, 0)
    return ((outgoing, outgoing_index, outgoing_tag), buffer_row)


def shards(
    shot_traces, slot_dest, slot_offset, block_count, amp_index, amp_table, dip_trace, dip_time
):
    traces = shot_traces[0]
    destination = slot_dest[0]
    position = slot_offset[0]
    index_rows = amp_index[0]
    live_count = block_count[0, 0]
    slot_total = traces.shape[0]
    block_len = traces.shape[1]
    sample_total = traces.shape[2]
    blocks_here = slot_total // 2
    taps_x = dip_trace.shape[1]
    taps_t = dip_time.shape[1]
    half_x = taps_x // 2
    line_count = lax.axis_size("rline")
    slot_ids = jnp.arange(slot_total, dtype=jnp.int32)
    live_mask = slot_ids < live_count
    capacity = (2 * blocks_here + line_count - 1) // line_count
    packed, buffer_row = pack_blocks(
        traces, index_rows, destination, position, live_mask, capacity, line_count
    )
    incoming, incoming_index, incoming_tag = (
        lax.all_to_all(packed[0], "rline", split_axis=0, concat_axis=0, tiled=True),
        lax.all_to_all(packed[1], "rline", split_axis=0, concat_axis=0, tiled=True),
        lax.all_to_all(packed[2], "rline", split_axis=0, concat_axis=0, tiled=True),
    )
    rows_in = line_count * capacity
    position_hit = incoming_tag[None, :] == (jnp.arange(blocks_here, dtype=jnp.int32) + 1)[:, None]
    row_of = jnp.sum(
        jnp.where(position_hit, jnp.arange(rows_in, dtype=jnp.int32)[None, :], 0), axis=1
    )
    line_blocks = jnp.take(incoming, row_of, axis=0)
    trace_index = jnp.take(incoming_index, row_of, axis=0).reshape(-1)
    amp_full = lax.all_gather(amp_table, "shot", axis=0, tiled=True)
    table_hit = trace_index[:, None] == jnp.arange(amp_full.shape[0], dtype=jnp.int32)[None, :]
    weights = jnp.sum(jnp.where(table_hit, amp_full[None, :], jnp.float32(0.0)), axis=1)
    receiver_line = line_blocks.reshape(blocks_here * block_len, sample_total)
    extended = extended_2(receiver_line, (("rline", 0),), half_x)
    tail_zeros = jnp.zeros((block_len - half_x, sample_total), jnp.bfloat16)
    padded = jnp.concatenate([extended, tail_zeros], axis=0)
    matrices = (
        band_matrix(dip_trace, block_len, block_len, 0),
        band_matrix(dip_trace, block_len, taps_x, block_len),
        band_matrix(dip_time, tile_len, tile_len, 0),
        band_matrix(dip_time, tile_len, taps_t, tile_len),
    )
    cleaned = lax.map(
        lambda block_idx: filter_block(padded, weights, block_idx, matrices),
        jnp.arange(blocks_here, dtype=jnp.int32),
    )
    returning = jnp.take(cleaned, jnp.maximum(incoming_tag - 1, 0), axis=0)
    returning = jnp.where((incoming_tag > 0)[:, None, None], returning, jnp.zeros((), jnp.bfloat16))
    returned = lax.all_to_all(returning, "rline", split_axis=0, concat_axis=0, tiled=True)
    result = jnp.take(returned, jnp.minimum(buffer_row, rows_in - 1), axis=0)
    result = jnp.where(live_mask[:, None, None], result, jnp.zeros((), jnp.bfloat16))
    return result[None]


def solution(mesh):
    in_specs = (
        P("shot", "rline", None, None),
        P("shot", "rline"),
        P("shot", "rline"),
        P("shot", "rline"),
        P("shot", "rline", None),
        P("shot"),
        P(),
        P(),
    )
    out_specs = P("shot", "rline", None, None)
    return jax.shard_map(shards, mesh=mesh, in_specs=in_specs, out_specs=out_specs, check_vma=False)
```

profile of v0, /device:TPU:32, one launch (start us, length us, event | category | flops | bytes accessed | tf_op | source)
XLA Modules:
  0.0 845.4 jit_solution(101710549481819221)
XLA Ops:
  4.7 8.1 all-to-all-start
  15.0 10.8 %gather_fusion.1 = bf16[32,128,2048]{2,1,0:T(8,128)(2,1)} fusion(bf16[18,128,2048]{2,1,0:T(8,128)(2,1)} %bitcast.152, s32[1024]{0:T(1024)S(1)} %pad_clamp_fusion.3), kind=kCustom, calls=%fused_computation.1 | custom fusion | bytes 33554560 | tf_op jit(solution)/shard_map/jit(_take)/gather | solution.py:83
  25.7 7.1 all-to-all-start.2
  32.8 14.3 %select_select_fusion.1 = bf16[32,128,2048]{2,1,0:T(8,128)(2,1)} fusion(bf16[32,128,2048]{2,1,0:T(8,128)(2,1)} %gather_fusion.1, pred[32]{0:T(512)(128)(4,1)S(1)} %compare_and_fusion.1, pred[32]{0:T(512)(128)(4,1)S(1)} %fusion.31), kind=kLoop, calls=%fused_computation.27 | loop fusion | flops 16777216 | bytes 33554496 | tf_op jit(solution)/shard_map/jit(_where)/select_n | solution.py:82
  47.1 7.4 all-to-all-start.1
  56.7 10.6 %all-gather = f32[8,1,128]{2,1,0:T(1,128)S(1)} all-gather(f32[1,1,128]{2,1,0:T(1,128)S(1)} %bitcast.159), channel_id=1, replica_groups=mesh['shot'=8,'rline'=16] {'shot'}, dimensions={0}, use_global_device_ids=true | all-gather | bytes 4608 | tf_op jit(solution)/shard_map/all_gather | solution.py:124
  69.7 283.4 %all-to-all-done.1 = bf16[32,128,2048]{2,1,0:T(8,128)(2,1)} async-done(((bf16[32,128,2048]{2,1,0:T(8,128)(2,1)}), bf16[32,128,2048]{2,1,0:T(8,128)(2,1)}, u32[]{:S(2)}, u32[]{:S(2)}) %all-to-all-start.1) | async-done | bytes 16777248 | tf_op jit(solution)/shard_map/all_to_all | solution.py:113
  353.1 9.5 %gather_fusion.2 = bf16[9,128,2048]{2,1,0:T(8,128)(2,1)} fusion(bf16[32,128,2048]{2,1,0:T(8,128)(2,1)} %all-to-all-done.1, s32[1024]{0:T(1024)S(1)} %pad_clamp_fusion.2), kind=kCustom, calls=%fused_computation.2 | custom fusion | bytes 9437220 | tf_op jit(solution)/shard_map/jit(_take)/gather | solution.py:122
  373.5 5.6 maximum_maximum_fusion
  379.1 143.9 %while.12 = (s32[]{:T(128)}, bf16[9,128,2048]{2,1,0:T(8,128)(2,1)}, s32[9]{0:T(128)S(1)}, bf16[1296,2048]{1,0:T(8,128)(2,1)}, f32[1152]{0:T(1024)S(1)}, /*index=...) while((s32[]{:T(128)}, bf16[9,128,2048]{2,1,0:T(8,128)(2,1)}, ...), condition=%wide.region_6.7_spmd, body=%wide.region_5.6_spmd.sunk | while | flops 1481900032 | bytes 46991640 | solution.py:137
  380.3 5.7 fusion.62
  386.1 4.7 fusion.63
  396.3 5.7 fusion.62
  402.1 4.7 fusion.63
  412.3 5.7 fusion.62
  428.3 5.7 fusion.62
  444.3 5.7 fusion.62
  450.0 4.7 fusion.63
  460.3 5.7 fusion.62
  466.0 4.7 fusion.63
  476.3 5.7 fusion.62
  482.0 4.7 fusion.63
  492.2 5.7 fusion.62
  498.0 4.7 fusion.63
  508.2 5.7 fusion.62
  514.0 4.7 fusion.63
  523.0 9.4 %gather_fusion.5 = bf16[32,128,2048]{2,1,0:T(8,128)(2,1)} fusion(bf16[9,128,2048]{2,1,0:T(8,128)(2,1)} %get-tuple-element.118, s32[1024]{0:T(1024)S(1)} %pad_clamp_fusion.1), kind=kCustom, calls=%fused_computation.5 | custom fusion | bytes 33554560 | tf_op jit(solution)/shard_map/jit(_take)/gather | solution.py:141
  532.4 14.3 %select_select_fusion = bf16[32,128,2048]{2,1,0:T(8,128)(2,1)} fusion(bf16[32,128,2048]{2,1,0:T(8,128)(2,1)} %gather_fusion.5, pred[32]{0:T(512)(128)(4,1)S(1)} %get-tuple-element.185, pred[32]{0:T(512)(128)(4,1)S(1)} %get-tuple-element.184), kind=kLoop, calls=%fused_computation.26 | loop fusion | flops 16777216 | bytes 33554496 | tf_op jit(solution)/shard_map/jit(_where)/select_n | solution.py:142
  546.7 8.5 %all-to-all-start.3 = ((bf16[32,128,2048]{2,1,0:T(8,128)(2,1)}), bf16[32,128,2048]{2,1,0:T(8,128)(2,1)}, u32[]{:S(2)}, u32[]{:S(2)}) async-start(bf16[32,128,2048]{2,1,0:T(8,128)(2,1)} %select_select_fusion), calls=%async_computation.3 | async-start | bytes 33554432 | tf_op jit(solution)/shard_map/all_to_all | solution.py:143
  555.2 270.8 %all-to-all-done.3 = bf16[32,128,2048]{2,1,0:T(8,128)(2,1)} async-done(((bf16[32,128,2048]{2,1,0:T(8,128)(2,1)}), bf16[32,128,2048]{2,1,0:T(8,128)(2,1)}, u32[]{:S(2)}, u32[]{:S(2)}) %all-to-all-start.3) | async-done | bytes 16777248 | tf_op jit(solution)/shard_map/all_to_all | solution.py:143
  826.0 10.9 %gather_fusion.6 = bf16[18,128,2048]{2,1,0:T(8,128)(2,1)} fusion(bf16[32,128,2048]{2,1,0:T(8,128)(2,1)} %all-to-all-done.3, s32[1024]{0:T(1024)S(1)} %pad_clamp_fusion), kind=kCustom, calls=%fused_computation.6 | custom fusion | bytes 18874440 | tf_op jit(solution)/shard_map/jit(_take)/gather | solution.py:144
  836.9 8.5 %fusion.16 = bf16[1,18,128,2048]{3,2,1,0:T(8,128)(2,1)} fusion(bf16[18,128,2048]{2,1,0:T(8,128)(2,1)} %gather_fusion.6, pred[18]{0:T(512)(128)(4,1)S(1)} %compare_and_fusion.3, pred[18]{0:T(512)(128)(4,1)S(1)} %iota_compare_fusion.23), kind=kLoop, calls=%fused_computation.29 | loop fusion | flops 9437184 | bytes 18874404 | tf_op jit(solution)/shard_map/jit(_where)/select_n | solution.py:145
  (165 shorter events, 74.1 us)
Async XLA Ops:
  0.0 55.0 %copy-start = (bf16[8,64]{1,0:T(8,128)(2,1)S(1)}, bf16[8,64]{1,0:T(8,128)(2,1)}, u32[]{:S(2)}) copy-start(bf16[8,64]{1,0:T(8,128)(2,1)} %param.17) | copy-start | bytes 3076
  4.7 21.0 %all-to-all-start = ((s32[16,2,1]{1,2,0:T(1,128)}), s32[16,2,1]{1,2,0:T(1,128)S(1)}, u32[]{:S(2)}, u32[]{:S(2)}) async-start(s32[16,2,1]{1,2,0:T(1,128)} %bitcast.20), calls=%async_computation | async-start | bytes 16384 | tf_op jit(solution)/shard_map/all_to_all | solution.py:115
  25.7 21.4 %all-to-all-start.2 = ((s32[16,2,128]{2,1,0:T(2,128)}), s32[16,2,128]{2,1,0:T(2,128)S(1)}, u32[]{:S(2)}, u32[]{:S(2)}) async-start(s32[16,2,128]{2,1,0:T(2,128)} %select_select_fusion.2), calls=%async_computation.2 | async-start | bytes 32768 | tf_op jit(solution)/shard_map/all_to_all | solution.py:114
  47.1 7.4 copy-start.4
  47.1 9.6 %copy-start.3 = (f32[128]{0:T(128)S(1)}, f32[128]{0:T(128)}, u32[]{:S(2)}) copy-start(f32[128]{0:T(128)} %param.15) | copy-start | bytes 1540
  47.1 306.0 %all-to-all-start.1 = ((bf16[32,128,2048]{2,1,0:T(8,128)(2,1)}), bf16[32,128,2048]{2,1,0:T(8,128)(2,1)}, u32[]{:S(2)}, u32[]{:S(2)}) async-start(bf16[32,128,2048]{2,1,0:T(8,128)(2,1)} %select_select_fusion.1), calls=%async_computation.1 | async-start | bytes 33554432 | tf_op jit(solution)/shard_map/all_to_all | solution.py:113
  365.4 6.8 collective-permute-start
  367.4 6.2 collective-permute-start.1
  546.7 8.5 %copy-start.2 = (s32[1,18]{1,0:T(1,128)S(1)}, s32[1,18]{1,0:T(1,128)}, u32[]{:S(2)}) copy-start(s32[1,18]{1,0:T(1,128)} %param.11) | copy-start | bytes 220
  546.7 279.3 %all-to-all-start.3 = ((bf16[32,128,2048]{2,1,0:T(8,128)(2,1)}), bf16[32,128,2048]{2,1,0:T(8,128)(2,1)}, u32[]{:S(2)}, u32[]{:S(2)}) async-start(bf16[32,128,2048]{2,1,0:T(8,128)(2,1)} %select_select_fusion), calls=%async_computation.3 | async-start | bytes 33554432 | tf_op jit(solution)/shard_map/all_to_all | solution.py:143
  826.0 19.5 %copy-start.1 = (bf16[8,64]{1,0:T(8,128)(2,1)S(1)}, bf16[8,64]{1,0:T(8,128)(2,1)}, u32[]{:S(2)}) copy-start(bf16[8,64]{1,0:T(8,128)(2,1)} %param.17) | copy-start | bytes 3076
where the time goes:
time: 852 us; the launch traced here: 845 us
  waiting for transfers between devices  556 us (65%)
  matrix products  107 us (13%)
  local copies, waits for them, and re-layouts  76.2 us (9%)
  other arithmetic  51.7 us (6%)
  starting transfers between devices  37 us (4%)
  blocking collectives  10.6 us (1%)
    all_to_all x1, waiting for transfers between devices, shards(): lax.all_to_all(packed[0], 'rline', split_axis=0, concat_axis=0, tiled=True)  283 us
    all_to_all x1, waiting for transfers between devices, shards(): lax.all_to_all(returning, 'rline', split_axis=0, concat_axis=0, tiled=True)  271 us
    dot_general x9, matrix products, filter_block(): jnp.einsum('ciu,ut->cit', trace_main, window[:block_len], preferred_eleme...  51.6 us
    dot_general x9, matrix products, filter_block(): jnp.einsum('ciu,ut->cit', trace_tail, window[block_len:], preferred_eleme...  42.6 us
  transfers between devices with their start and end apart: 6, of which 3 were waited for; matrix products, arithmetic and copies ran while one was open for 4% of the time, Pallas kernels for 0%

commit v1 on v0

v1 whole, which is shorter than its diff:
```python
import functools

import jax
import jax.numpy as jnp
from jax import lax
from jax.experimental import pallas as pl
from jax.experimental.pallas import tpu as pltpu
from jax.sharding import PartitionSpec as P

BF16 = jnp.bfloat16
F32 = jnp.float32
EDGE = 16
TILE = 256
VMEM_LIMIT = 56 * 2**20


def time_matrix(dip_time):
    dips, taps = dip_time.shape
    row = lax.broadcasted_iota(jnp.int32, (256, 128), 0)
    col = lax.broadcasted_iota(jnp.int32, (256, 128), 1)
    hit = (row - col)[None] == jnp.arange(taps, dtype=jnp.int32)[:, None, None]
    values = dip_time.astype(F32)[:, :, None, None]
    band = jnp.sum(jnp.where(hit[None], values, F32(0.0)), axis=1).astype(BF16)
    zero = jnp.zeros((dips, 128, 128), BF16)
    main = jnp.concatenate([band, jnp.concatenate([zero, band[:, :128]], axis=1)], axis=2)
    tail = jnp.concatenate([zero, band[:, 128:]], axis=2)
    return jnp.concatenate([main.reshape(dips * 256, 256), tail.reshape(dips * 128, 256)], axis=0)


def trace_matrix(dip_trace, starts, width):
    dips, taps = dip_trace.shape
    rows = starts.shape[0]
    col = lax.broadcasted_iota(jnp.int32, (rows, width), 1)
    hit = (col - starts[:, None])[None] == jnp.arange(taps, dtype=jnp.int32)[:, None, None]
    values = dip_trace.astype(F32)[:, :, None, None]
    band = jnp.sum(jnp.where(hit[None], values, F32(0.0)), axis=1).astype(BF16)
    return band.reshape(dips * rows, width)


def time_lhs(tp, dips, rows, tile):
    base = tile * TILE
    parts = [tp[c * rows : (c + 1) * rows, base : base + 256] for c in range(dips)]
    parts += [tp[c * rows : (c + 1) * rows, base + 256 : base + 384] for c in range(dips)]
    return jnp.concatenate(parts, axis=1)


def interior_kernel(dips, half_t, count, x, w, xi, m, *refs):
    o, shifted, tp = refs[-3:]
    rows = x.shape[1] - 2 * EDGE
    samples = x.shape[2]
    slot = pl.program_id(0) + count[1]

    @pl.when(pl.program_id(0) == 0)
    def _():
        shifted[...] = jnp.zeros_like(shifted)

    @pl.when(slot < count[0])
    def _():
        shifted[:, half_t : half_t + samples] = x[0]
        for lo in range(0, samples + 128, TILE):
            hi = min(lo + TILE, samples + 128)
            tp[:, lo:hi] = jnp.dot(
                xi[...], shifted[:, lo:hi], preferred_element_type=F32
            ).astype(BF16)
        for tile in range(samples // TILE):
            cols = slice(tile * TILE, (tile + 1) * TILE)
            noise = jnp.dot(
                time_lhs(tp, dips, rows, tile), m[...], preferred_element_type=F32
            )
            weight = jnp.concatenate([w[0, EDGE : EDGE + rows]] * 2, axis=1)
            center = x[0, EDGE : EDGE + rows, cols].astype(F32)
            o[0, EDGE : EDGE + rows, cols] = (center - weight * noise).astype(BF16)

    @pl.when(slot >= count[0])
    def _():
        o[...] = jnp.zeros_like(o)


def interior(count, x, w, xi, m, start, steps, out=None):
    slots, block, samples = x.shape
    dips = m.shape[0] // 384
    fetch = lambda i, n: (jnp.minimum(i + n[1], jnp.maximum(n[0] - 1, 0)), 0, 0)
    in_specs = [
        pl.BlockSpec((1, block, samples), fetch),
        pl.BlockSpec((1, block, 128), fetch),
        pl.BlockSpec(xi.shape, lambda i, n: (0, 0)),
        pl.BlockSpec(m.shape, lambda i, n: (0, 0)),
    ]
    args = [jnp.stack([count, jnp.int32(start)]), x, w, xi, m]
    aliases = {}
    if out is not None:
        in_specs.append(pl.BlockSpec(memory_space=pl.ANY))
        args.append(out)
        aliases = {5: 0}
    return pl.pallas_call(
        functools.partial(interior_kernel, dips, 32),
        out_shape=jax.ShapeDtypeStruct(x.shape, BF16),
        grid_spec=pltpu.PrefetchScalarGridSpec(
            num_scalar_prefetch=1,
            grid=(steps,),
            in_specs=in_specs,
            out_specs=pl.BlockSpec((1, block, samples), lambda i, n: (i + n[1], 0, 0)),
            scratch_shapes=[
                pltpu.VMEM((block, samples + 128), BF16),
                pltpu.VMEM((xi.shape[0], samples + 128), BF16),
            ],
        ),
        input_output_aliases=aliases,
        compiler_params=pltpu.CompilerParams(
            dimension_semantics=("arbitrary",), vmem_limit_bytes=VMEM_LIMIT
        ),
        cost_estimate=pl.CostEstimate(
            flops=steps * 8_000_000_000, bytes_accessed=steps * 2**20, transcendentals=0
        ),
        name="interior",
    )(*args)


def edge_kernel(dips, half_t, groups, count, xt, xb, halo, w, xe, m, _, o, shifted, tp, res, sems):
    g = pl.program_id(0)
    per = xt.shape[0]
    samples = xt.shape[2]
    rows = per * 2 * EDGE
    n_slices = halo.shape[0]
    live = g * per < count[0]

    def copies(group):
        slots = pl.ds(group * per, per)
        return (
            pltpu.make_async_copy(
                res.at[group, :, pl.ds(0, EDGE)], o.at[slots, pl.ds(0, EDGE)], sems.at[group, 0]
            ),
            pltpu.make_async_copy(
                res.at[group, :, pl.ds(EDGE, EDGE)],
                o.at[slots, pl.ds(128 - EDGE, EDGE)],
                sems.at[group, 1],
            ),
        )

    @pl.when(g == 0)
    def _():
        shifted[...] = jnp.zeros_like(shifted)

    @pl.when(live)
    def _():
        for i in range(per):
            above = jnp.concatenate([halo[s, i, :EDGE] for s in range(n_slices)], axis=1)
            below = jnp.concatenate([halo[s, i, EDGE:] for s in range(n_slices)], axis=1)
            here = slice(half_t, half_t + samples)
            shifted[i, 0:16, here] = above
            shifted[i, 16:48, here] = xt[i]
            shifted[i, 48:80, here] = xb[i]
            shifted[i, 80:96, here] = below
            for lo in range(0, samples + 128, TILE):
                hi = min(lo + TILE, samples + 128)
                part = jnp.dot(xe[...], shifted[i, :, lo:hi], preferred_element_type=F32)
                part = part.astype(BF16)
                for c in range(dips):
                    tp[c * rows + i * 32 : c * rows + i * 32 + 32, lo:hi] = part[c * 32 : c * 32 + 32]
        for tile in range(samples // TILE):
            cols = slice(tile * TILE, (tile + 1) * TILE)
            noise = jnp.dot(
                time_lhs(tp, dips, rows, tile), m[...], preferred_element_type=F32
            )
            for i in range(per):
                keep = g * per + i < count[0]
                top = noise[i * 32 : i * 32 + 16]
                bottom = noise[i * 32 + 16 : i * 32 + 32]
                wt = jnp.concatenate([w[i, :EDGE]] * 2, axis=1)
                wb = jnp.concatenate([w[i, 128 - EDGE :]] * 2, axis=1)
                top = xt[i, :EDGE, cols].astype(F32) - wt * top
                bottom = xb[i, EDGE:, cols].astype(F32) - wb * bottom
                res[g, i, :EDGE, cols] = jnp.where(keep, top, 0.0).astype(BF16)
                res[g, i, EDGE:, cols] = jnp.where(keep, bottom, 0.0).astype(BF16)
        for copy in copies(g):
            copy.start()

    @pl.when(g == groups - 1)
    def _():
        for group in range(groups):

            @pl.when(group * per < count[0])
            def _():
                for copy in copies(group):
                    copy.wait()


def edges(count, x, halo, w, xe, m, out, per=6):
    slots, block, samples = x.shape
    dips = m.shape[0] // 384
    groups = slots // per
    last = lambda g, n: jnp.minimum(g, jnp.maximum(n[0] - 1, 0) // per)
    return pl.pallas_call(
        functools.partial(edge_kernel, dips, 32, groups),
        out_shape=jax.ShapeDtypeStruct(x.shape, BF16),
        grid_spec=pltpu.PrefetchScalarGridSpec(
            num_scalar_prefetch=1,
            grid=(groups,),
            in_specs=[
                pl.BlockSpec((per, 32, samples), lambda g, n: (last(g, n), 0, 0)),
                pl.BlockSpec((per, 32, samples), lambda g, n: (last(g, n), 3, 0)),
                pl.BlockSpec((halo.shape[0], per, 32, 128), lambda g, n: (0, last(g, n), 0, 0)),
                pl.BlockSpec((per, block, 128), lambda g, n: (last(g, n), 0, 0)),
                pl.BlockSpec(xe.shape, lambda g, n: (0, 0)),
                pl.BlockSpec(m.shape, lambda g, n: (0, 0)),
                pl.BlockSpec(memory_space=pl.ANY),
            ],
            out_specs=pl.BlockSpec(memory_space=pl.ANY),
            scratch_shapes=[
                pltpu.VMEM((per, 96, samples + 128), BF16),
                pltpu.VMEM((dips * per * 32, samples + 128), BF16),
                pltpu.VMEM((groups, per, 32, samples), BF16),
                pltpu.SemaphoreType.DMA((groups, 2)),
            ],
        ),
        input_output_aliases={7: 0},
        compiler_params=pltpu.CompilerParams(
            dimension_semantics=("arbitrary",), vmem_limit_bytes=VMEM_LIMIT
        ),
        cost_estimate=pl.CostEstimate(
            flops=8_000_000_000, bytes_accessed=2**23, transcendentals=0
        ),
        name="edges",
    )(count.reshape(1), x, x, halo, w, xe, m, out)


def permute_kernel(before, after, x, o):
    total = x.shape[0]

    def step(q, _):
        a = before[q]
        b = after[q]
        above = x[jnp.maximum(a, 0), EDGE:]
        below = x[jnp.maximum(b, 0), :EDGE]
        o[q, :EDGE] = jnp.where(a >= 0, above, jnp.zeros_like(above))
        o[q, EDGE:] = jnp.where(b >= 0, below, jnp.zeros_like(below))
        return 0

    lax.fori_loop(0, total, step, 0, unroll=8)


def permute(before, after, x):
    return pl.pallas_call(
        permute_kernel,
        out_shape=jax.ShapeDtypeStruct(x.shape, BF16),
        grid_spec=pltpu.PrefetchScalarGridSpec(
            num_scalar_prefetch=2,
            grid=(1,),
            in_specs=[pl.BlockSpec(x.shape, lambda i, a, b: (0, 0, 0))],
            out_specs=pl.BlockSpec(x.shape, lambda i, a, b: (0, 0, 0)),
        ),
        compiler_params=pltpu.CompilerParams(vmem_limit_bytes=VMEM_LIMIT),
        cost_estimate=pl.CostEstimate(flops=0, bytes_accessed=2**23, transcendentals=0),
        name="permute",
    )(before, after, x)


def shards(
    shot_traces, slot_dest, slot_offset, block_count, amp_index, amp_table, dip_trace, dip_time
):
    x = shot_traces[0]
    slots, block, samples = x.shape
    lines = lax.axis_size("rline")
    per_line = slots // 2
    width = samples // lines
    count = block_count[0, 0]
    slot_ids = jnp.arange(slots, dtype=jnp.int32)
    place = jnp.where(slot_ids < count, slot_dest[0] * per_line + slot_offset[0], -2)

    ends = jnp.concatenate([x[:, :EDGE], x[:, block - EDGE :]], axis=1)
    ends = ends.reshape(slots, 2 * EDGE, lines, width).transpose(2, 0, 1, 3)
    slice_ends = lax.all_to_all(ends, "rline", split_axis=0, concat_axis=0, tiled=True)

    places = lax.all_gather(place, "rline", axis=0, tiled=True)
    amps = lax.all_gather(amp_table, "shot", axis=0, tiled=True)
    ids = jnp.arange(places.shape[0], dtype=jnp.int32)[None, :]
    difference = places[None, :] - places[:, None]
    known = (places >= 0)[:, None] & (places >= 0)[None, :]
    before = jnp.max(jnp.where(known & (difference == -1), ids, -1), axis=1)
    after = jnp.max(jnp.where(known & (difference == 1), ids, -1), axis=1)

    table_hit = amp_index[0][:, :, None] == jnp.arange(amps.shape[0], dtype=jnp.int32)
    weight = jnp.sum(jnp.where(table_hit, amps, F32(0.0)), axis=2)
    weight = jnp.broadcast_to(weight[:, :, None], (slots, block, 128))

    m = time_matrix(dip_time)
    rows = jnp.arange(block - 2 * EDGE, dtype=jnp.int32)
    xi = trace_matrix(dip_trace, rows, block)
    edge_rows = jnp.arange(2 * EDGE, dtype=jnp.int32)
    xe = trace_matrix(dip_trace, jnp.where(edge_rows < EDGE, edge_rows, edge_rows + 32), 96)

    half = slots // 2
    out = interior(count, x, weight, xi, m, 0, half)
    flat = slice_ends.reshape(lines * slots, 2 * EDGE, width)
    moved = permute(before, after, flat).reshape(lines, slots, 2 * EDGE, width)
    halo = lax.all_to_all(moved, "rline", split_axis=0, concat_axis=0, tiled=True)
    out = interior(count, x, weight, xi, m, half, half, out)
    out = edges(count, x, halo, weight, xe, m, out)
    return out[None]


def solution(mesh):
    in_specs = (
        P("shot", "rline", None, None),
        P("shot", "rline"),
        P("shot", "rline"),
        P("shot", "rline"),
        P("shot", "rline", None),
        P("shot"),
        P(),
        P(),
    )
    out_specs = P("shot", "rline", None, None)
    return jax.shard_map(shards, mesh=mesh, in_specs=in_specs, out_specs=out_specs, check_vma=False)
```

time: 852 us -> 152 us (0.18)
  the two profiles are of different devices: /device:TPU:32 before, /device:TPU:104 now
where the time goes in v1:
time: 152 us; the launch traced here: 151 us
  Pallas kernels  85.7 us (56%)
  blocking collectives  23.9 us (16%)
  other arithmetic  19.7 us (13%)
  starting transfers between devices  13.1 us (9%)
  local copies, waits for them, and re-layouts  6.74 us (4%)
  between operations  1.64 us (1%)
    pallas_call x2, Pallas kernels, interior(): pl.pallas_call(functools.partial(interior_kernel, dips, 32), out_shape=ja...  63.5 us
    pallas_call x1, Pallas kernels, edges(): pl.pallas_call(functools.partial(edge_kernel, dips, 32, groups), out_shap...  16.8 us
    unnamed x1, blocking collectives  13.4 us
    all_gather x1, blocking collectives, shards(): amps = lax.all_gather(amp_table, 'shot', axis=0, tiled=True)  10.5 us
    reduce_sum x1, other arithmetic, time_matrix(): band = jnp.sum(jnp.where(hit[None], values, F32(0.0)), axis=1).astype(BF16)  7.32 us
    all_to_all x1, starting transfers between devices, shards(): lax.all_to_all(ends, 'rline', split_axis=0, concat_axis=0, tiled=True)  7.04 us
    all_to_all x1, starting transfers between devices, shards(): lax.all_to_all(moved, 'rline', split_axis=0, concat_axis=0, tiled=True)  6.03 us
    pallas_call x1, Pallas kernels, permute(): pl.pallas_call(permute_kernel, out_shape=jax.ShapeDtypeStruct(x.shape, BF...  5.37 us
  transfers between devices with their start and end apart: 2, of which 0 were waited for; matrix products, arithmetic and copies ran while one was open for 13% of the time, Pallas kernels for 42%

profile of v1, /device:TPU:104, one launch (start us, length us, event | category | flops | bytes accessed | tf_op | source)
XLA Modules:
  0.0 150.8 jit_solution(4588300994294048944)
XLA Ops:
  0.0 1.8 %fusion.3 = (bf16[18,16,2048]{2,1,0:T(8,128)(2,1)S(1)}, bf16[18,16,2048]{2,1,0:T(8,128)(2,1)S(1)}) fusion(bf16[18,128,2048]{2,1,0:T(8,128)(2,1)} %bitcast.29), kind=kLoop, calls=%fused_computation.30 | loop fusion | bytes 4718592 | tf_op jit(solution)/shard_map/slice | solution.py:270
  1.8 2.0 %bitcast_bitcast_fusion = bf16[16,18,32,128]{3,2,1,0:T(8,128)(2,1)} fusion(bf16[18,16,2048]{2,1,0:T(8,128)(2,1)S(1)} %get-tuple-element.8, bf16[18,16,2048]{2,1,0:T(8,128)(2,1)S(1)} %get-tuple-element.7), kind=kLoop, calls=%fused_computation.6 | loop fusion | flops 4718592 | bytes 4718592 | tf_op jit(solution)/shard_map/transpose | solution.py:271
  3.8 7.0 %all-to-all-start = ((bf16[16,18,32,128]{3,2,1,0:T(8,128)(2,1)}), bf16[16,18,32,128]{3,2,1,0:T(8,128)(2,1)S(1)}, u32[]{:S(2)}, u32[]{:S(2)}) async-start(bf16[16,18,32,128]{3,2,1,0:T(8,128)(2,1)} %bitcast_bitcast_fusion), calls=%async_computation | async-start | bytes 4718592 | tf_op jit(solution)/shard_map/all_to_all | solution.py:272
  10.9 1.2 iota_compare_fusion.1
  12.2 0.0 copy-start.4
  12.2 0.0 copy-start.7
  12.2 0.0 copy-start.6
  12.2 7.3 %select_reduce_fusion = bf16[8,256,128]{2,1,0:T(8,128)(2,1)S(1)} fusion(f32[8,64]{1,0:T(8,128)S(1)} %convert_element_type.27, pred[64,256,128]{2,1,0:T(8,128)(4,1)S(1)} %iota_compare_fusion.1), kind=kLoop, calls=%fused_computation | loop fusion | flops 33292288 | bytes 2623488 | tf_op jit(solution)/shard_map/reduce_sum | solution.py:23
  19.6 0.1 fusion.1
  20.4 10.5 %all-gather = f32[8,1,128]{2,1,0:T(1,128)S(1)} all-gather(f32[1,1,128]{2,1,0:T(1,128)S(1)} %bitcast.43), channel_id=1, replica_groups=mesh['shot'=8,'rline'=16] {'shot'}, dimensions={0}, use_global_device_ids=true | all-gather | bytes 4608 | tf_op jit(solution)/shard_map/all_gather | solution.py:275
  30.9 0.2 iota_compare_fusion.3
  31.2 1.3 pad_maximum_fusion.m
  32.4 0.6 pad_add_fusion.1.count
  33.0 1.4 select_reduce_fusion.2
  34.5 2.4 %select_reduce_fusion.1 = bf16[8,96,128]{2,1,0:T(8,128)(2,1)} fusion(f32[8,32]{1,0:T(8,128)S(1)} %convert_element_type.24, pred[32,96,128]{2,1,0:T(8,128)(4,1)S(1)} %iota_compare_fusion.3), kind=kLoop, calls=%fused_computation.1 | loop fusion | flops 6193152 | bytes 590848 | tf_op jit(solution)/shard_map/reduce_sum | solution.py:36
  36.9 1.4 broadcast_in_dim.123.w
  38.3 31.8 %interior.2.refs_0_ = bf16[18,128,2048]{2,1,0:T(8,128)(2,1)} custom-call(s32[2]{0:T(128)} %pad_add_fusion.1.count, bf16[18,128,2048]{2,1,0:T(8,128)(2,1)} %bitcast.30, f32[18,128,128]{2,1,0:T(8,128)} %broadcast_in_dim.123.w, bf16[768,128]{1,0:T(8,128)(2,1)} %bitcast.39, bf16[3072,256]{1,0:T(8,128)(2,1)} %pad_maximum_fusion.m), custom_call_target="tpu_custom_call" | custom-call | flops 71999995904 | bytes 9437184 | tf_op jit(solution)/shard_map/interior/pallas_call | solution.py:95
  70.1 0.6 dynamic-slice
  71.4 0.1 fusion.2
  71.5 13.4 %all-reduce.2 = s32[288]{0:T(512)S(1)} all-reduce(s32[288]{0:T(512)S(1)} %fusion.2), channel_id=1, replica_groups=mesh['shot'=8,'rline'=16] {'rline'}, use_global_device_ids=true, to_apply=%add.2 | all-reduce | flops 288 | bytes 2304
  84.9 0.7 pad_add_fusion.count
  85.6 1.0 select_reduce_fusion.4
  86.6 1.4 copy-done.1
  88.0 5.4 %permute.1 = bf16[288,32,128]{2,1,0:T(8,128)(2,1)} custom-call(s32[288]{0:T(512)} %get-tuple-element.6.before, s32[288]{0:T(512)} %get-tuple-element.5.after, bf16[288,32,128]{2,1,0:T(8,128)(2,1)} %bitcast.34), custom_call_target="tpu_custom_call" | custom-call | bytes 8388608 | tf_op jit(solution)/shard_map/permute/pallas_call | solution.py:243
  93.4 6.0 %all-to-all-start.1 = ((bf16[16,18,32,128]{3,2,1,0:T(8,128)(2,1)}), bf16[16,18,32,128]{3,2,1,0:T(8,128)(2,1)S(1)}, u32[]{:S(2)}, u32[]{:S(2)}) async-start(bf16[16,18,32,128]{3,2,1,0:T(8,128)(2,1)} %bitcast.35), calls=%async_computation.1 | async-start | bytes 4718592 | tf_op jit(solution)/shard_map/all_to_all | solution.py:296
  99.4 31.7 %interior.3._ = bf16[18,128,2048]{2,1,0:T(8,128)(2,1)} custom-call(s32[2]{0:T(128)} %pad_add_fusion.count, bf16[18,128,2048]{2,1,0:T(8,128)(2,1)} %bitcast.31, f32[18,128,128]{2,1,0:T(8,128)} %broadcast_in_dim.123.w, bf16[768,128]{1,0:T(8,128)(2,1)} %bitcast.40, bf16[3072,256]{1,0:T(8,128)(2,1)} %pad_maximum_fusion.m, ...), custom_call_target="tpu_custom_call", output_to_operand_aliasing={{}: (5, {})} | custom-call | flops 71999995904 | bytes 9437184 | tf_op jit(solution)/shard_map/interior/pallas_call | solution.py:95
  131.1 0.1 iota_subtract_fusion.2
  131.2 0.1 iota_compare_fusion.4
  131.2 1.1 select_reduce_fusion.3
  132.4 0.0 all-to-all-done.1.halo
  132.4 1.4 copy-done
  133.8 16.8 %edges.1 = bf16[18,128,2048]{2,1,0:T(8,128)(2,1)} custom-call(s32[1]{0:T(128)} %bitcast.26.count, bf16[18,128,2048]{2,1,0:T(8,128)(2,1)} %bitcast.32, bf16[18,128,2048]{2,1,0:T(8,128)(2,1)} %bitcast.33, bf16[16,18,32,128]{3,2,1,0:T(8,128)(2,1)} %copy-done, f32[18,128,128]{2,1,0:T(8,128)} %broadcast_in_dim.123.w, ...), custom_call_target="tpu_custom_call", output_to_operand_aliasing={{}: (7, {})} | custom-call | flops 8000000000 | bytes 8388608 | tf_op jit(solution)/shard_map/edges/pallas_call | solution.py:193
  (28 shorter events, 0.2 us)
Async XLA Ops:
  3.8 82.8 %all-to-all-start = ((bf16[16,18,32,128]{3,2,1,0:T(8,128)(2,1)}), bf16[16,18,32,128]{3,2,1,0:T(8,128)(2,1)S(1)}, u32[]{:S(2)}, u32[]{:S(2)}) async-start(bf16[16,18,32,128]{3,2,1,0:T(8,128)(2,1)} %bitcast_bitcast_fusion), calls=%async_computation | async-start | bytes 4718592 | tf_op jit(solution)/shard_map/all_to_all | solution.py:272
  10.9 1.3 copy-start.5
  12.2 8.2 %copy-start.4 = (s32[1,18,128]{2,0,1:T(1,128)S(1)}, s32[1,18,128]{2,0,1:T(1,128)}, u32[]{:S(2)}) copy-start(s32[1,18,128]{2,0,1:T(1,128)} %param.12) | copy-start | bytes 27652
  12.2 8.2 %copy-start.7 = (f32[128]{0:T(128)S(1)}, f32[128]{0:T(128)}, u32[]{:S(2)}) copy-start(f32[128]{0:T(128)} %param.13) | copy-start | bytes 1540
  12.2 18.7 %copy-start.6 = (bf16[8,32]{1,0:T(8,128)(2,1)S(1)}, bf16[8,32]{1,0:T(8,128)(2,1)}, u32[]{:S(2)}) copy-start(bf16[8,32]{1,0:T(8,128)(2,1)} %param.14) | copy-start | bytes 1540
  30.9 6.0 %copy-start.2 = (f32[8,32]{1,0:T(8,128)}, f32[8,32]{1,0:T(8,128)S(1)}, u32[]{:S(2)}) copy-start(f32[8,32]{1,0:T(8,128)S(1)} %convert_element_type.24) | copy-start | bytes 3076
  38.3 31.8 %copy-start.10 = (u32[128]{0:T(128)S(1)}, u32[128]{0:T(128)}, u32[]{:S(2)}) copy-start(u32[128]{0:T(128)} %constant.36) | copy-start | bytes 1540
  38.3 33.1 %copy-start.8 = (s32[1,18]{1,0:T(1,128)S(1)}, s32[1,18]{1,0:T(1,128)}, u32[]{:S(2)}) copy-start(s32[1,18]{1,0:T(1,128)} %param.10) | copy-start | bytes 220
  38.3 33.1 %copy-start.9 = (s32[1,18]{1,0:T(1,128)S(1)}, s32[1,18]{1,0:T(1,128)}, u32[]{:S(2)}) copy-start(s32[1,18]{1,0:T(1,128)} %param.9) | copy-start | bytes 220
  86.6 1.4 copy-start.1
  93.4 39.0 %all-to-all-start.1 = ((bf16[16,18,32,128]{3,2,1,0:T(8,128)(2,1)}), bf16[16,18,32,128]{3,2,1,0:T(8,128)(2,1)S(1)}, u32[]{:S(2)}, u32[]{:S(2)}) async-start(bf16[16,18,32,128]{3,2,1,0:T(8,128)(2,1)} %bitcast.35), calls=%async_computation.1 | async-start | bytes 4718592 | tf_op jit(solution)/shard_map/all_to_all | solution.py:296
  99.4 31.9 %copy-start.3 = (f32[8,32]{1,0:T(8,128)S(1)}, f32[8,32]{1,0:T(8,128)}, u32[]{:S(2)}) copy-start(f32[8,32]{1,0:T(8,128)} %copy-done.2) | copy-start | bytes 3076
  132.4 1.4 copy-start

commit v2 on v1

v2 whole, which is shorter than its diff:
```python
import functools

import jax
import jax.numpy as jnp
from jax import lax
from jax.experimental import pallas as pl
from jax.experimental.pallas import tpu as pltpu
from jax.sharding import PartitionSpec as P

BF16 = jnp.bfloat16
F32 = jnp.float32
EDGE = 16
TILE = 256
HALF_T = 32
PAIR_K = 640
VMEM_LIMIT = 56 * 2**20
FIRST = 7


def params(limit=VMEM_LIMIT):
    return pltpu.CompilerParams(dimension_semantics=("arbitrary",), vmem_limit_bytes=limit)


def cost(flops, bytes_accessed):
    return pl.CostEstimate(flops=flops, bytes_accessed=bytes_accessed, transcendentals=0)


def dip_order(dips):
    return list(range(0, dips, 2)) + list(range(1, dips, 2))


def matrices_kernel(taps_x, taps_t, m, xi, xe):
    dips = taps_x.shape[0]
    row = lax.broadcasted_iota(jnp.int32, (TILE, TILE), 0)
    col = lax.broadcasted_iota(jnp.int32, (TILE, TILE), 1)
    for c in range(dips):
        base = jnp.broadcast_to(taps_t[c : c + 1], (TILE, TILE))
        band = pltpu.roll(base, 0, 1, stride=1, stride_axis=0)
        at = c * (PAIR_K // 2)
        m[at : at + TILE] = jnp.where(col <= row, band, 0.0).astype(BF16)
        m[at + TILE : at + PAIR_K // 2] = jnp.where(col > row, band, 0.0)[:64].astype(BF16)
    rows = xi.shape[0] // dips
    for i, c in enumerate(dip_order(dips)):
        base = jnp.broadcast_to(taps_x[c : c + 1], (rows, 128))
        band = pltpu.roll(base, 0, 1, stride=1, stride_axis=0)
        xi[i * rows : (i + 1) * rows] = band.astype(BF16)
        xe[i * 32 : i * 32 + 16] = band[:16, :96].astype(BF16)
        xe[i * 32 + 16 : i * 32 + 32] = band[48:64, :96].astype(BF16)


def matrices(dip_trace, dip_time, rows):
    dips, taps = dip_time.shape
    taps_x = jnp.pad(dip_trace.astype(F32), ((0, 0), (0, 128 - dip_trace.shape[1])))
    taps_t = dip_time.astype(F32)
    gap = jnp.zeros((dips, TILE - taps), F32)
    taps_t = jnp.concatenate([taps_t[:, :1], gap, taps_t[:, :0:-1]], axis=1)
    return pl.pallas_call(
        matrices_kernel,
        out_shape=(
            jax.ShapeDtypeStruct((dips * PAIR_K // 2, TILE), BF16),
            jax.ShapeDtypeStruct((dips * rows, 128), BF16),
            jax.ShapeDtypeStruct((dips * 32, 96), BF16),
        ),
        compiler_params=pltpu.CompilerParams(vmem_limit_bytes=16 * 2**20),
        cost_estimate=cost(0, 2**21),
        name="matrices",
    )(taps_x, taps_t)


def time_lhs(tp, dips, rows, tile):
    base = tile * TILE
    low = lax.broadcasted_iota(jnp.int32, (rows, 128), 1) < 64
    parts = []
    for pair in range(dips // 2):
        even = pl.ds(pair * rows, rows)
        odd = pl.ds((dips // 2 + pair) * rows, rows)
        parts.append(tp[even, base : base + 256])
        parts.append(jnp.where(low, tp[even, base + 256 : base + 384], tp[odd, base : base + 128]))
        parts.append(tp[odd, base + 128 : base + 384])
    return jnp.concatenate(parts, axis=1)


def noise_tiles(tp, m, dips, rows, tiles):
    lhs = jnp.concatenate([time_lhs(tp, dips, rows, tile) for tile in tiles], axis=0)
    noise = jnp.dot(lhs, m[...], preferred_element_type=F32)
    return [noise[k * rows : (k + 1) * rows] for k in range(len(tiles))]


def column_tiles(samples):
    return [(lo, min(lo + TILE, samples + 128)) for lo in range(0, samples + 128, TILE)]


def interior_kernel(dips, count, x, w, xi, m, *refs):
    o, shifted, tp = refs[-3:]
    rows = x.shape[1] - 2 * EDGE
    samples = x.shape[2]
    half = dips // 2 * rows
    slot = pl.program_id(0) + count[1]

    @pl.when(pl.program_id(0) == 0)
    def _():
        shifted[...] = jnp.zeros_like(shifted)

    @pl.when(slot < count[0])
    def _():
        shifted[0, :, HALF_T : HALF_T + samples] = x[0]
        shifted[1, :, HALF_T + 64 : HALF_T + 64 + samples] = x[0]
        for k in range(2):
            for lo, hi in column_tiles(samples):
                tp[k * half : (k + 1) * half, lo:hi] = jnp.dot(
                    xi[k * half : (k + 1) * half],
                    shifted[k, :, lo:hi],
                    preferred_element_type=F32,
                ).astype(BF16)
        weight = jnp.concatenate([w[0, EDGE : EDGE + rows]] * 2, axis=1)
        for first in range(0, samples // TILE, 2):
            tiles = (first, first + 1)
            for tile, noise in zip(tiles, noise_tiles(tp, m, dips, rows, tiles)):
                cols = slice(tile * TILE, (tile + 1) * TILE)
                center = x[0, EDGE : EDGE + rows, cols].astype(F32)
                o[0, EDGE : EDGE + rows, cols] = (center - weight * noise).astype(BF16)

    @pl.when(slot >= count[0])
    def _():
        o[...] = jnp.zeros_like(o)


def interior(count, x, w, xi, m, start, steps, out=None):
    slots, block, samples = x.shape
    dips = m.shape[0] * 2 // PAIR_K
    fetch = lambda i, n: (jnp.minimum(i + n[1], jnp.maximum(n[0] - 1, 0)), 0, 0)
    in_specs = [
        pl.BlockSpec((1, block, samples), fetch),
        pl.BlockSpec((1, block, 128), fetch),
        pl.BlockSpec(xi.shape, lambda i, n: (0, 0)),
        pl.BlockSpec(m.shape, lambda i, n: (0, 0)),
    ]
    args = [jnp.stack([count, jnp.int32(start)]), x, w, xi, m]
    aliases = {}
    if out is not None:
        in_specs.append(pl.BlockSpec(memory_space=pl.ANY))
        args.append(out)
        aliases = {5: 0}
    return pl.pallas_call(
        functools.partial(interior_kernel, dips),
        out_shape=jax.ShapeDtypeStruct(x.shape, BF16),
        grid_spec=pltpu.PrefetchScalarGridSpec(
            num_scalar_prefetch=1,
            grid=(steps,),
            in_specs=in_specs,
            out_specs=pl.BlockSpec((1, block, samples), lambda i, n: (i + n[1], 0, 0)),
            scratch_shapes=[
                pltpu.VMEM((2, block, samples + 128), BF16),
                pltpu.VMEM((xi.shape[0], samples + 128), BF16),
            ],
        ),
        input_output_aliases=aliases,
        compiler_params=params(),
        cost_estimate=cost(steps * 2_000_000_000, steps * 2**20),
        name="interior",
    )(*args)


def edge_kernel(dips, groups, count, xt, xb, halo, w, xe, m, _, o, shifted, tp, res, sems):
    g = pl.program_id(0)
    per = xt.shape[0]
    samples = xt.shape[2]
    rows = per * 2 * EDGE
    n_slices = halo.shape[0]
    half = xe.shape[0] // 2
    live = g * per < count[0]

    def copies(group):
        slots = pl.ds(group * per, per)
        return (
            pltpu.make_async_copy(
                res.at[group, :, pl.ds(0, EDGE)], o.at[slots, pl.ds(0, EDGE)], sems.at[group, 0]
            ),
            pltpu.make_async_copy(
                res.at[group, :, pl.ds(EDGE, EDGE)],
                o.at[slots, pl.ds(128 - EDGE, EDGE)],
                sems.at[group, 1],
            ),
        )

    @pl.when(g == 0)
    def _():
        shifted[...] = jnp.zeros_like(shifted)

    @pl.when(live)
    def _():
        for i in range(per):
            above = [halo[s, i * 32 : i * 32 + EDGE] for s in range(n_slices)]
            below = [halo[s, i * 32 + EDGE : i * 32 + 32] for s in range(n_slices)]
            above = jnp.concatenate(above, axis=1)
            below = jnp.concatenate(below, axis=1)
            for k in range(2):
                here = slice(HALF_T + 64 * k, HALF_T + 64 * k + samples)
                shifted[k, i, 0:16, here] = above
                shifted[k, i, 16:48, here] = xt[i]
                shifted[k, i, 48:80, here] = xb[i]
                shifted[k, i, 80:96, here] = below
                for lo, hi in column_tiles(samples):
                    part = jnp.dot(
                        xe[k * half : (k + 1) * half],
                        shifted[k, i, :, lo:hi],
                        preferred_element_type=F32,
                    ).astype(BF16)
                    for c in range(dips // 2):
                        at = (k * dips // 2 + c) * rows + i * 32
                        tp[at : at + 32, lo:hi] = part[c * 32 : c * 32 + 32]
        for tile in range(samples // TILE):
            cols = slice(tile * TILE, (tile + 1) * TILE)
            [noise] = noise_tiles(tp, m, dips, rows, (tile,))
            for i in range(per):
                keep = g * per + i < count[0]
                top = noise[i * 32 : i * 32 + 16]
                bottom = noise[i * 32 + 16 : i * 32 + 32]
                wt = jnp.concatenate([w[i, :EDGE]] * 2, axis=1)
                wb = jnp.concatenate([w[i, 128 - EDGE :]] * 2, axis=1)
                top = xt[i, :EDGE, cols].astype(F32) - wt * top
                bottom = xb[i, EDGE:, cols].astype(F32) - wb * bottom
                res[g, i, :EDGE, cols] = jnp.where(keep, top, 0.0).astype(BF16)
                res[g, i, EDGE:, cols] = jnp.where(keep, bottom, 0.0).astype(BF16)
        for copy in copies(g):
            copy.start()

    @pl.when(g == groups - 1)
    def _():
        for group in range(groups):

            @pl.when(group * per < count[0])
            def _():
                for copy in copies(group):
                    copy.wait()


def edges(count, x, halo, w, xe, m, out, per=6):
    slots, block, samples = x.shape
    dips = m.shape[0] * 2 // PAIR_K
    groups = slots // per
    last = lambda g, n: jnp.minimum(g, jnp.maximum(n[0] - 1, 0) // per)
    return pl.pallas_call(
        functools.partial(edge_kernel, dips, groups),
        out_shape=jax.ShapeDtypeStruct(x.shape, BF16),
        grid_spec=pltpu.PrefetchScalarGridSpec(
            num_scalar_prefetch=1,
            grid=(groups,),
            in_specs=[
                pl.BlockSpec((per, 32, samples), lambda g, n: (last(g, n), 0, 0)),
                pl.BlockSpec((per, 32, samples), lambda g, n: (last(g, n), 3, 0)),
                pl.BlockSpec((halo.shape[0], per * 32, 128), lambda g, n: (0, last(g, n), 0)),
                pl.BlockSpec((per, block, 128), lambda g, n: (last(g, n), 0, 0)),
                pl.BlockSpec(xe.shape, lambda g, n: (0, 0)),
                pl.BlockSpec(m.shape, lambda g, n: (0, 0)),
                pl.BlockSpec(memory_space=pl.ANY),
            ],
            out_specs=pl.BlockSpec(memory_space=pl.ANY),
            scratch_shapes=[
                pltpu.VMEM((2, per, 96, samples + 128), BF16),
                pltpu.VMEM((dips * per * 32, samples + 128), BF16),
                pltpu.VMEM((groups, per, 32, samples), BF16),
                pltpu.SemaphoreType.DMA((groups, 2)),
            ],
        ),
        input_output_aliases={7: 0},
        compiler_params=params(),
        cost_estimate=cost(8_000_000_000, 2**23),
        name="edges",
    )(count.reshape(1), x, x, halo, w, xe, m, out)


def payload_kernel(per_line, count, dest, offset, xt, xb, o):
    slots = xt.shape[0]
    slot = lax.broadcasted_iota(jnp.int32, (1, slots), 1)
    place = jnp.where(slot < count[0, 0], dest[...] * per_line + offset[...], -2)
    place = jnp.broadcast_to(place.astype(F32), (EDGE, slots)).astype(BF16)
    for s in range(o.shape[0]):
        cols = slice(s * 128, (s + 1) * 128)
        for i in range(slots):
            o[s, i * 32 : i * 32 + EDGE] = xt[i, :, cols]
            o[s, i * 32 + EDGE : i * 32 + 32] = xb[i, :, cols]
        o[s, slots * 32 :, 0:slots] = place


def payload(block_count, slot_dest, slot_offset, x, steps=4):
    slots, block, samples = x.shape
    slices = samples // 128
    per = slices // steps
    return pl.pallas_call(
        functools.partial(payload_kernel, slots // 2),
        out_shape=jax.ShapeDtypeStruct((slices, slots * 32 + EDGE, 128), BF16),
        grid=(steps,),
        in_specs=[
            pl.BlockSpec(memory_space=pltpu.SMEM),
            pl.BlockSpec((1, slots), lambda i: (0, 0)),
            pl.BlockSpec((1, slots), lambda i: (0, 0)),
            pl.BlockSpec((slots, EDGE, per * 128), lambda i: (0, 0, i)),
            pl.BlockSpec((slots, EDGE, per * 128), lambda i: (0, block // EDGE - 1, i)),
        ],
        out_specs=pl.BlockSpec((per, slots * 32 + EDGE, 128), lambda i: (i, 0, 0)),
        compiler_params=params(16 * 2**20),
        cost_estimate=cost(0, 2**22),
        name="payload",
    )(block_count, slot_dest, slot_offset, x, x)


def permute_kernel(slots, x, o, places, table, where, sem):
    sources = places.shape[0]
    stride = slots * 32 + EDGE
    for s in range(sources):
        row = x[s * stride + slots * 32 : (s + 1) * stride]
        places[s : s + 1] = row.astype(F32)[:1].astype(jnp.int32)
    copy = pltpu.make_async_copy(places, table, sem)
    copy.start()
    copy.wait()
    total = sources * (slots // 2)
    where[0] = -1
    where[total + 1] = -1

    def fill(s, _):
        for i in range(slots):
            p = table[s, i]
            where[jnp.where(p < 0, total + 2, p + 1)] = s * stride + i * 32
        return 0

    lax.fori_loop(0, sources, fill, 0)

    def move(s, _):
        for i in range(slots):
            p = jnp.maximum(table[s, i], 0)
            a = where[p]
            b = where[p + 2]
            above = x[pl.ds(pl.multiple_of(jnp.maximum(a, 0) + EDGE, EDGE), EDGE)]
            below = x[pl.ds(pl.multiple_of(jnp.maximum(b, 0), EDGE), EDGE)]
            o[s, i * 32 : i * 32 + EDGE] = jnp.where(a >= 0, above, jnp.zeros_like(above))
            o[s, i * 32 + EDGE : i * 32 + 32] = jnp.where(b >= 0, below, jnp.zeros_like(below))
        return 0

    lax.fori_loop(0, sources, move, 0)


def permute(x, slots):
    sources, rows, width = x.shape
    total = sources * (slots // 2)
    return pl.pallas_call(
        functools.partial(permute_kernel, slots),
        out_shape=jax.ShapeDtypeStruct((sources, slots * 32, width), BF16),
        in_specs=[pl.BlockSpec(memory_space=pltpu.VMEM)],
        out_specs=pl.BlockSpec(memory_space=pltpu.VMEM),
        scratch_shapes=[
            pltpu.VMEM((sources, 128), jnp.int32),
            pltpu.SMEM((sources, 128), jnp.int32),
            pltpu.SMEM((total + 3,), jnp.int32),
            pltpu.SemaphoreType.DMA,
        ],
        compiler_params=pltpu.CompilerParams(vmem_limit_bytes=16 * 2**20),
        cost_estimate=cost(0, 2**23),
        name="permute",
    )(x.reshape(sources * rows, width))


def shards(
    shot_traces, slot_dest, slot_offset, block_count, amp_index, amp_table, dip_trace, dip_time
):
    x = shot_traces[0]
    slots, block, samples = x.shape
    count = block_count[0, 0]

    ends = payload(block_count, slot_dest, slot_offset, x)
    ends = lax.all_to_all(ends, "rline", split_axis=0, concat_axis=0, tiled=True)

    amps = lax.all_gather(amp_table, "shot", axis=0, tiled=True)
    table_hit = amp_index[0][:, :, None] == jnp.arange(amps.shape[0], dtype=jnp.int32)
    weight = jnp.sum(jnp.where(table_hit, amps, F32(0.0)), axis=2)
    weight = jnp.broadcast_to(weight[:, :, None], (slots, block, 128))
    m, xi, xe = matrices(dip_trace, dip_time, block - 2 * EDGE)

    out = interior(count, x, weight, xi, m, 0, FIRST)
    moved = permute(ends, slots)
    halo = lax.all_to_all(moved, "rline", split_axis=0, concat_axis=0, tiled=True)
    out = interior(count, x, weight, xi, m, FIRST, slots - FIRST, out)
    out = edges(count, x, halo, weight, xe, m, out)
    return out[None]


def solution(mesh):
    in_specs = (
        P("shot", "rline", None, None),
        P("shot", "rline"),
        P("shot", "rline"),
        P("shot", "rline"),
        P("shot", "rline", None),
        P("shot"),
        P(),
        P(),
    )
    out_specs = P("shot", "rline", None, None)
    return jax.shard_map(shards, mesh=mesh, in_specs=in_specs, out_specs=out_specs, check_vma=False)
```

time: 152 us -> 124 us (0.82)
  the two profiles are of different devices: /device:TPU:104 before, /device:TPU:32 now
where the time goes in v2:
time: 124 us
  Pallas kernels  65.7 us (53%)
  waiting for transfers between devices  17.5 us (14%)
  local copies, waits for them, and re-layouts  13.3 us (11%)
  starting transfers between devices  13 us (10%)
  blocking collectives  10.5 us (8%)
  other arithmetic  2.85 us (2%)
    pallas_call x2, Pallas kernels, interior(): pl.pallas_call(functools.partial(interior_kernel, dips), out_shape=jax.Sh...  45.8 us
    all_to_all x1, waiting for transfers between devices, shards(): lax.all_to_all(ends, 'rline', split_axis=0, concat_axis=0, tiled=True)  17.5 us
    pallas_call x1, Pallas kernels, edges(): pl.pallas_call(functools.partial(edge_kernel, dips, groups), out_shape=ja...  15.7 us
    unnamed x27, local copies, waits for them, and re-layouts  11.6 us
    all_gather x1, blocking collectives, shards(): amps = lax.all_gather(amp_table, 'shot', axis=0, tiled=True)  10.5 us
    all_to_all x1, starting transfers between devices, shards(): lax.all_to_all(ends, 'rline', split_axis=0, concat_axis=0, tiled=True)  8.06 us
    all_to_all x1, starting transfers between devices, shards(): lax.all_to_all(moved, 'rline', split_axis=0, concat_axis=0, tiled=True)  4.97 us
    pallas_call x1, Pallas kernels, permute(): pl.pallas_call(functools.partial(permute_kernel, slots), out_shape=jax.Sh...  3.32 us
  transfers between devices with their start and end apart: 2, of which 1 were waited for; matrix products, arithmetic and copies ran while one was open for 4% of the time, Pallas kernels for 37%

profile of v2, /device:TPU:32, one launch (start us, length us, event | category | flops | bytes accessed | tf_op | source)
XLA Modules:
  0.0 123.6 jit_solution(15162619255214800090)
XLA Ops:
  0.7 0.0 copy-start
  0.7 3.7 %copy-done = bf16[1,18,128,2048]{3,2,1,0:T(8,128)(2,1)S(1)} copy-done((bf16[1,18,128,2048]{3,2,1,0:T(8,128)(2,1)S(1)}, bf16[1,18,128,2048]{3,2,1,0:T(8,128)(2,1)}, u32[]{:S(2)}) %copy-start) | copy-done | bytes 9437208
  4.3 0.7 copy-done.5
  5.0 0.7 copy-done.6
  5.7 0.7 payload.1
  6.3 0.0 copy-start.1
  6.4 1.4 %copy-done.1 = bf16[16,592,128]{2,1,0:T(8,128)(2,1)} copy-done((bf16[16,592,128]{2,1,0:T(8,128)(2,1)}, bf16[16,592,128]{2,1,0:T(8,128)(2,1)S(1)}, u32[]{:S(2)}) %copy-start.1) | copy-done | bytes 2424856
  7.8 8.1 %all-to-all-start = ((bf16[16,592,128]{2,1,0:T(8,128)(2,1)}), bf16[16,592,128]{2,1,0:T(8,128)(2,1)S(1)}, u32[]{:S(2)}, u32[]{:S(2)}) async-start(bf16[16,592,128]{2,1,0:T(8,128)(2,1)} %copy-done.1), calls=%async_computation | async-start | bytes 4849664 | tf_op jit(solution)/shard_map/all_to_all | solution.py:371
  15.8 0.1 slice.7
  15.9 0.1 rev.3
  16.0 0.0 copy-done.10
  16.0 0.1 pad.13.clone
  16.1 0.1 pad_maximum_fusion.taps_t
  16.2 0.3 matrices.1
  16.5 1.1 copy-done.3
  17.6 0.6 copy-done.4
  18.2 0.7 copy-done.7
  18.9 0.0 copy-done.12
  18.9 10.5 %all-gather = f32[8,1,128]{2,1,0:T(1,128)S(1)} all-gather(f32[1,1,128]{2,1,0:T(1,128)S(1)} %bitcast.21), channel_id=1, replica_groups=mesh['shot'=8,'rline'=16] {'shot'}, dimensions={0}, use_global_device_ids=true | all-gather | bytes 4608 | tf_op jit(solution)/shard_map/all_gather | solution.py:373
  29.4 0.7 pad_add_fusion.1.count
  30.0 1.4 %select_reduce_fusion = f32[18,128]{1,0:T(8,128)S(1)} fusion(f32[1024]{0:T(1024)S(1)} %bitcast.20, s32[18,128]{1,0:T(8,128)S(1)} %bitcast.19), kind=kLoop, calls=%fused_computation | loop fusion | flops 7075584 | bytes 22528 | tf_op jit(solution)/shard_map/reduce_sum | solution.py:375
  31.5 17.5 %all-to-all-done = bf16[16,592,128]{2,1,0:T(8,128)(2,1)S(1)} async-done(((bf16[16,592,128]{2,1,0:T(8,128)(2,1)}), bf16[16,592,128]{2,1,0:T(8,128)(2,1)S(1)}, u32[]{:S(2)}, u32[]{:S(2)}) %all-to-all-start) | async-done | bytes 2424864 | tf_op jit(solution)/shard_map/all_to_all | solution.py:371
  49.0 3.3 %permute.1 = bf16[16,576,128]{2,1,0:T(8,128)(2,1)S(1)} custom-call(bf16[9472,128]{1,0:T(8,128)(2,1)S(1)} %bitcast.18), custom_call_target="tpu_custom_call" | custom-call | bytes 8388608 | tf_op jit(solution)/shard_map/permute/pallas_call | solution.py:346
  52.3 1.4 %copy-done.2 = bf16[16,576,128]{2,1,0:T(8,128)(2,1)} copy-done((bf16[16,576,128]{2,1,0:T(8,128)(2,1)}, bf16[16,576,128]{2,1,0:T(8,128)(2,1)S(1)}, u32[]{:S(2)}) %copy-start.2) | copy-done | bytes 2359320
  53.7 5.0 %all-to-all-start.1 = ((bf16[16,576,128]{2,1,0:T(8,128)(2,1)}), bf16[16,576,128]{2,1,0:T(8,128)(2,1)S(1)}, u32[]{:S(2)}, u32[]{:S(2)}) async-start(bf16[16,576,128]{2,1,0:T(8,128)(2,1)} %copy-done.2), calls=%async_computation.1 | async-start | bytes 4718592 | tf_op jit(solution)/shard_map/all_to_all | solution.py:381
  58.7 1.4 %broadcast_in_dim.23.w = f32[18,128,128]{2,1,0:T(8,128)} broadcast(f32[18,128]{1,0:T(8,128)S(1)} %select_reduce_fusion), dimensions={0,1} | broadcast | bytes 1188864 | tf_op jit(solution)/shard_map/broadcast_in_dim | solution.py:376
  60.1 18.5 %interior.2.refs_0_ = bf16[18,128,2048]{2,1,0:T(8,128)(2,1)} custom-call(s32[2]{0:T(128)} %pad_add_fusion.1.count, bf16[18,128,2048]{2,1,0:T(8,128)(2,1)} %bitcast.12, f32[18,128,128]{2,1,0:T(8,128)} %broadcast_in_dim.23.w, bf16[768,128]{1,0:T(8,128)(2,1)} %copy-done.7, bf16[2560,256]{1,0:T(8,128)(2,1)} %copy-done.3), custom_call_target="tpu_custom_call" | custom-call | flops 14000000000 | bytes 7340032 | tf_op jit(solution)/shard_map/interior/pallas_call | solution.py:144
  78.6 0.7 pad_add_fusion.count
  79.3 27.3 %interior.3._ = bf16[18,128,2048]{2,1,0:T(8,128)(2,1)} custom-call(s32[2]{0:T(128)} %pad_add_fusion.count, bf16[18,128,2048]{2,1,0:T(8,128)(2,1)} %bitcast.13, f32[18,128,128]{2,1,0:T(8,128)} %broadcast_in_dim.23.w, bf16[768,128]{1,0:T(8,128)(2,1)} %copy-done.7, bf16[2560,256]{1,0:T(8,128)(2,1)} %copy-done.3, ...), custom_call_target="tpu_custom_call", output_to_operand_aliasing={{}: (5, {})} | custom-call | flops 22000001024 | bytes 11534336 | tf_op jit(solution)/shard_map/interior/pallas_call | solution.py:144
  106.5 0.0 all-to-all-done.1.halo
  106.6 1.4 %copy-done.8 = bf16[16,576,128]{2,1,0:T(8,128)(2,1)} copy-done((bf16[16,576,128]{2,1,0:T(8,128)(2,1)}, bf16[16,576,128]{2,1,0:T(8,128)(2,1)S(1)}, u32[]{:S(2)}) %copy-start.8) | copy-done | bytes 2359320
  108.0 15.7 %edges.1 = bf16[18,128,2048]{2,1,0:T(8,128)(2,1)} custom-call(s32[1]{0:T(128)} %bitcast.10.count, bf16[18,128,2048]{2,1,0:T(8,128)(2,1)} %bitcast.14, bf16[18,128,2048]{2,1,0:T(8,128)(2,1)} %bitcast.15, bf16[16,576,128]{2,1,0:T(8,128)(2,1)} %copy-done.8, f32[18,128,128]{2,1,0:T(8,128)} %broadcast_in_dim.23.w, ...), custom_call_target="tpu_custom_call", output_to_operand_aliasing={{}: (7, {})} | custom-call | flops 8000000000 | bytes 8388608 | tf_op jit(solution)/shard_map/edges/pallas_call | solution.py:243
  (17 shorter events, 0.0 us)
Async XLA Ops:
  0.7 3.7 %copy-start = (bf16[1,18,128,2048]{3,2,1,0:T(8,128)(2,1)S(1)}, bf16[1,18,128,2048]{3,2,1,0:T(8,128)(2,1)}, u32[]{:S(2)}) copy-start(bf16[1,18,128,2048]{3,2,1,0:T(8,128)(2,1)} %param.8) | copy-start | bytes 28311556
  4.3 0.7 copy-start.5
  5.0 0.7 copy-start.6
  5.6 10.2 %copy-start.9 = (bf16[8,64]{1,0:T(8,128)(2,1)S(1)}, bf16[8,64]{1,0:T(8,128)(2,1)}, u32[]{:S(2)}) copy-start(bf16[8,64]{1,0:T(8,128)(2,1)} %param.15) | copy-start | bytes 3076
  5.6 10.3 %copy-start.10 = (s32[1,18,128]{2,0,1:T(1,128)S(1)}, s32[1,18,128]{2,0,1:T(1,128)}, u32[]{:S(2)}) copy-start(s32[1,18,128]{2,0,1:T(1,128)} %param.12) | copy-start | bytes 27652
  5.7 10.4 %copy-start.11 = (bf16[8,32]{1,0:T(8,128)(2,1)S(1)}, bf16[8,32]{1,0:T(8,128)(2,1)}, u32[]{:S(2)}) copy-start(bf16[8,32]{1,0:T(8,128)(2,1)} %param.14) | copy-start | bytes 1540
  5.7 13.2 %copy-start.12 = (f32[128]{0:T(128)S(1)}, f32[128]{0:T(128)}, u32[]{:S(2)}) copy-start(f32[128]{0:T(128)} %param.13) | copy-start | bytes 1540
  6.3 1.4 %copy-start.1 = (bf16[16,592,128]{2,1,0:T(8,128)(2,1)}, bf16[16,592,128]{2,1,0:T(8,128)(2,1)S(1)}, u32[]{:S(2)}) copy-start(bf16[16,592,128]{2,1,0:T(8,128)(2,1)S(1)} %payload.1) | copy-start | bytes 7274500
  7.8 41.2 %all-to-all-start = ((bf16[16,592,128]{2,1,0:T(8,128)(2,1)}), bf16[16,592,128]{2,1,0:T(8,128)(2,1)S(1)}, u32[]{:S(2)}, u32[]{:S(2)}) async-start(bf16[16,592,128]{2,1,0:T(8,128)(2,1)} %copy-done.1), calls=%async_computation | async-start | bytes 4849664 | tf_op jit(solution)/shard_map/all_to_all | solution.py:371
  16.5 1.1 copy-start.3
  17.6 0.6 copy-start.4
  18.2 0.7 copy-start.7
  52.3 1.4 %copy-start.2 = (bf16[16,576,128]{2,1,0:T(8,128)(2,1)}, bf16[16,576,128]{2,1,0:T(8,128)(2,1)S(1)}, u32[]{:S(2)}) copy-start(bf16[16,576,128]{2,1,0:T(8,128)(2,1)S(1)} %permute.1) | copy-start | bytes 7077892
  53.7 52.8 %all-to-all-start.1 = ((bf16[16,576,128]{2,1,0:T(8,128)(2,1)}), bf16[16,576,128]{2,1,0:T(8,128)(2,1)S(1)}, u32[]{:S(2)}, u32[]{:S(2)}) async-start(bf16[16,576,128]{2,1,0:T(8,128)(2,1)} %copy-done.2), calls=%async_computation.1 | async-start | bytes 4718592 | tf_op jit(solution)/shard_map/all_to_all | solution.py:381
  106.6 1.4 %copy-start.8 = (bf16[16,576,128]{2,1,0:T(8,128)(2,1)}, bf16[16,576,128]{2,1,0:T(8,128)(2,1)S(1)}, u32[]{:S(2)}) copy-start(bf16[16,576,128]{2,1,0:T(8,128)(2,1)S(1)} %all-to-all-done.1.halo) | copy-start | bytes 7077892

commit v3 on v2

--- a/solution.py
+++ b/solution.py
@@ -14,7 +14,8 @@
 HALF_T = 32
 PAIR_K = 640
 VMEM_LIMIT = 56 * 2**20
-FIRST = 7
+EDGE_VMEM = 52 * 2**20
+FIRST = 6
 
 
 def params(limit=VMEM_LIMIT):
@@ -264,7 +265,7 @@
             ],
         ),
         input_output_aliases={7: 0},
-        compiler_params=params(),
+        compiler_params=params(EDGE_VMEM),
         cost_estimate=cost(8_000_000_000, 2**23),
         name="edges",
     )(count.reshape(1), x, x, halo, w, xe, m, out)
@@ -299,7 +300,7 @@
             pl.BlockSpec((slots, EDGE, per * 128), lambda i: (0, block // EDGE - 1, i)),
         ],
         out_specs=pl.BlockSpec((per, slots * 32 + EDGE, 128), lambda i: (i, 0, 0)),
-        compiler_params=params(16 * 2**20),
+        compiler_params=params(),
         cost_estimate=cost(0, 2**22),
         name="payload",
     )(block_count, slot_dest, slot_offset, x, x)
@@ -377,6 +378,7 @@
     m, xi, xe = matrices(dip_trace, dip_time, block - 2 * EDGE)
 
     out = interior(count, x, weight, xi, m, 0, FIRST)
+    ends, out = lax.optimization_barrier((ends, out))
     moved = permute(ends, slots)
     halo = lax.all_to_all(moved, "rline", split_axis=0, concat_axis=0, tiled=True)
     out = interior(count, x, weight, xi, m, FIRST, slots - FIRST, out)

time: 124 us -> 107 us (0.86)
  waiting for transfers between devices: 17.5 us -> 2.77 us
  local copies, waits for them, and re-layouts: 13.3 us -> 4.85 us
  Pallas kernels: 65.7 us -> 69.1 us
  starting transfers between devices: 13 us -> 15.3 us
    all_to_all x1, waiting for transfers between devices: 17.5 us -> 0.01 us  [shards(): lax.all_to_all(ends, 'rline', split_axis=0, concat_axis=0, tiled=True)]
    unnamed x27 -> x17, local copies, waits for them, and re-layouts: 11.6 us -> 3.21 us
    pallas_call x1, Pallas kernels: 0.68 us -> 4.03 us  [payload(): pl.pallas_call(functools.partial(payload_kernel, slots // 2), out_shape=j...]
    all_to_all x1, waiting for transfers between devices: 0.01 us -> 2.77 us  [shards(): lax.all_to_all(moved, 'rline', split_axis=0, concat_axis=0, tiled=True)]
    all_to_all x1, starting transfers between devices: 4.97 us -> 7.22 us  [shards(): lax.all_to_all(moved, 'rline', split_axis=0, concat_axis=0, tiled=True)]
  transfers between devices with their start and end apart: 2 -> 2, of which waited for: 1 -> 1; matrix products, arithmetic and copies ran while one was open for 4% -> 4% of each run, Pallas kernels for 37% -> 44%
where the time goes in v3:
time: 107 us; the launch traced here: 106 us
  Pallas kernels  69.1 us (65%)
  starting transfers between devices  15.3 us (14%)
  blocking collectives  10.5 us (10%)
  local copies, waits for them, and re-layouts  4.85 us (5%)
  other arithmetic  2.82 us (3%)
  waiting for transfers between devices  2.77 us (3%)
    pallas_call x2, Pallas kernels, interior(): pl.pallas_call(functools.partial(interior_kernel, dips), out_shape=jax.Sh...  45.9 us
    pallas_call x1, Pallas kernels, edges(): pl.pallas_call(functools.partial(edge_kernel, dips, groups), out_shape=ja...  15.5 us
    all_gather x1, blocking collectives, shards(): amps = lax.all_gather(amp_table, 'shot', axis=0, tiled=True)  10.5 us
    all_to_all x1, starting transfers between devices, shards(): lax.all_to_all(ends, 'rline', split_axis=0, concat_axis=0, tiled=True)  8.06 us
    all_to_all x1, starting transfers between devices, shards(): lax.all_to_all(moved, 'rline', split_axis=0, concat_axis=0, tiled=True)  7.22 us
    pallas_call x1, Pallas kernels, payload(): pl.pallas_call(functools.partial(payload_kernel, slots // 2), out_shape=j...  4.03 us
    pallas_call x1, Pallas kernels, permute(): pl.pallas_call(functools.partial(permute_kernel, slots), out_shape=jax.Sh...  3.32 us
    unnamed x17, local copies, waits for them, and re-layouts  3.21 us
  transfers between devices with their start and end apart: 2, of which 1 were waited for; matrix products, arithmetic and copies ran while one was open for 4% of the time, Pallas kernels for 44%

profile of v3, /device:TPU:32, one launch (start us, length us, event | category | flops | bytes accessed | tf_op | source)
XLA Modules:
  0.0 106.0 jit_solution(8205622351489638123)
XLA Ops:
  0.7 0.0 copy-start.4
  0.7 0.0 copy-start.5
  0.7 0.0 copy-start.6
  0.7 0.0 copy-start.7
  0.7 4.0 %payload.1 = bf16[16,592,128]{2,1,0:T(8,128)(2,1)} custom-call(s32[1,1]{1,0:T(1,128)} %copy.16.count, s32[1,18]{1,0:T(1,128)} %dest.1, s32[1,18]{1,0:T(1,128)} %offset.1, bf16[18,128,2048]{2,1,0:T(8,128)(2,1)} %bitcast.13, bf16[18,128,2048]{2,1,0:T(8,128)(2,1)} %bitcast.14), custom_call_target="tpu_custom_call" | custom-call | bytes 4194304 | tf_op jit(solution)/shard_map/payload/pallas_call | solution.py:291
  4.7 8.1 %all-to-all-start = ((bf16[16,592,128]{2,1,0:T(8,128)(2,1)}), bf16[16,592,128]{2,1,0:T(8,128)(2,1)S(1)}, u32[]{:S(2)}, u32[]{:S(2)}) async-start(bf16[16,592,128]{2,1,0:T(8,128)(2,1)} %payload.1), calls=%async_computation | async-start | bytes 4849664 | tf_op jit(solution)/shard_map/all_to_all | solution.py:372
  12.8 0.0 copy-done.4
  12.8 0.1 slice.7
  12.9 0.1 rev.3
  12.9 0.0 copy-done.5
  13.0 0.1 pad.11.clone
  13.0 0.0 copy-done.6
  13.0 0.1 pad_maximum_fusion.taps_t
  13.1 0.3 matrices.1
  13.4 0.0 copy-start.2
  13.5 1.1 %copy-done.2 = bf16[2560,256]{1,0:T(8,128)(2,1)} copy-done((bf16[2560,256]{1,0:T(8,128)(2,1)}, bf16[2560,256]{1,0:T(8,128)(2,1)S(1)}, u32[]{:S(2)}) %copy-start.2) | copy-done | bytes 1310744
  14.6 0.7 copy-done.3
  15.2 0.0 copy-done.7
  15.2 10.5 %all-gather = f32[8,1,128]{2,1,0:T(1,128)S(1)} all-gather(f32[1,1,128]{2,1,0:T(1,128)S(1)} %bitcast.21), channel_id=1, replica_groups=mesh['shot'=8,'rline'=16] {'shot'}, dimensions={0}, use_global_device_ids=true | all-gather | bytes 4608 | tf_op jit(solution)/shard_map/all_gather | solution.py:374
  25.7 0.7 pad_add_fusion.count
  26.4 0.7 pad_add_fusion.1.count
  27.0 1.4 %select_reduce_fusion = f32[18,128]{1,0:T(8,128)S(1)} fusion(f32[1024]{0:T(1024)S(1)} %bitcast.20, s32[18,128]{1,0:T(8,128)S(1)} %bitcast.19), kind=kLoop, calls=%fused_computation | loop fusion | flops 7075584 | bytes 22528 | tf_op jit(solution)/shard_map/reduce_sum | solution.py:376
  28.5 1.4 %broadcast_in_dim.23.w = f32[18,128,128]{2,1,0:T(8,128)} broadcast(f32[18,128]{1,0:T(8,128)S(1)} %select_reduce_fusion), dimensions={0,1} | broadcast | bytes 1188864 | tf_op jit(solution)/shard_map/broadcast_in_dim | solution.py:377
  29.9 16.3 %interior.2.refs_0_ = bf16[18,128,2048]{2,1,0:T(8,128)(2,1)} custom-call(s32[2]{0:T(128)} %pad_add_fusion.count, bf16[18,128,2048]{2,1,0:T(8,128)(2,1)} %bitcast.15, f32[18,128,128]{2,1,0:T(8,128)} %broadcast_in_dim.23.w, bf16[768,128]{1,0:T(8,128)(2,1)} %copy-done.3, bf16[2560,256]{1,0:T(8,128)(2,1)} %copy-done.2), custom_call_target="tpu_custom_call" | custom-call | flops 12000000000 | bytes 6291456 | tf_op jit(solution)/shard_map/interior/pallas_call | solution.py:145
  46.2 0.0 all-to-all-done
  46.2 3.3 %permute.1 = bf16[16,576,128]{2,1,0:T(8,128)(2,1)S(1)} custom-call(bf16[9472,128]{1,0:T(8,128)(2,1)S(1)} %bitcast.12), custom_call_target="tpu_custom_call" | custom-call | bytes 8388608 | tf_op jit(solution)/shard_map/permute/pallas_call | solution.py:347
  49.5 0.0 copy-start
  49.5 1.4 %copy-done = bf16[16,576,128]{2,1,0:T(8,128)(2,1)} copy-done((bf16[16,576,128]{2,1,0:T(8,128)(2,1)}, bf16[16,576,128]{2,1,0:T(8,128)(2,1)S(1)}, u32[]{:S(2)}) %copy-start) | copy-done | bytes 2359320
  50.9 7.2 %all-to-all-start.1 = ((bf16[16,576,128]{2,1,0:T(8,128)(2,1)}), bf16[16,576,128]{2,1,0:T(8,128)(2,1)}, u32[]{:S(2)}, u32[]{:S(2)}) async-start(bf16[16,576,128]{2,1,0:T(8,128)(2,1)} %copy-done), calls=%async_computation.1 | async-start | bytes 4718592 | tf_op jit(solution)/shard_map/all_to_all | solution.py:383
  58.1 29.6 %interior.3._ = bf16[18,128,2048]{2,1,0:T(8,128)(2,1)} custom-call(s32[2]{0:T(128)} %pad_add_fusion.1.count, bf16[18,128,2048]{2,1,0:T(8,128)(2,1)} %bitcast.16, f32[18,128,128]{2,1,0:T(8,128)} %broadcast_in_dim.23.w, bf16[768,128]{1,0:T(8,128)(2,1)} %copy-done.3, bf16[2560,256]{1,0:T(8,128)(2,1)} %copy-done.2, ...), custom_call_target="tpu_custom_call", output_to_operand_aliasing={{}: (5, {})} | custom-call | flops 24000000000 | bytes 12582912 | tf_op jit(solution)/shard_map/interior/pallas_call | solution.py:145
  87.8 2.8 %all-to-all-done.1.halo = bf16[16,576,128]{2,1,0:T(8,128)(2,1)} async-done(((bf16[16,576,128]{2,1,0:T(8,128)(2,1)}), bf16[16,576,128]{2,1,0:T(8,128)(2,1)}, u32[]{:S(2)}, u32[]{:S(2)}) %all-to-all-start.1) | async-done | bytes 2359328 | tf_op jit(solution)/shard_map/all_to_all | solution.py:383
  90.5 15.5 %edges.1 = bf16[18,128,2048]{2,1,0:T(8,128)(2,1)} custom-call(s32[1]{0:T(128)} %bitcast.10.count, bf16[18,128,2048]{2,1,0:T(8,128)(2,1)} %bitcast.17, bf16[18,128,2048]{2,1,0:T(8,128)(2,1)} %bitcast.18, bf16[16,576,128]{2,1,0:T(8,128)(2,1)} %all-to-all-done.1.halo, f32[18,128,128]{2,1,0:T(8,128)S(1)} %copy-done.1, ...), custom_call_target="tpu_custom_call", output_to_operand_aliasing={{}: (7, {})} | custom-call | flops 8000000000 | bytes 8388608 | tf_op jit(solution)/shard_map/edges/pallas_call | solution.py:244
  (7 shorter events, 0.0 us)
Async XLA Ops:
  0.7 12.1 %copy-start.4 = (bf16[8,64]{1,0:T(8,128)(2,1)S(1)}, bf16[8,64]{1,0:T(8,128)(2,1)}, u32[]{:S(2)}) copy-start(bf16[8,64]{1,0:T(8,128)(2,1)} %param.15) | copy-start | bytes 3076
  0.7 12.3 %copy-start.5 = (s32[1,18,128]{2,0,1:T(1,128)S(1)}, s32[1,18,128]{2,0,1:T(1,128)}, u32[]{:S(2)}) copy-start(s32[1,18,128]{2,0,1:T(1,128)} %param.12) | copy-start | bytes 27652
  0.7 12.4 %copy-start.6 = (bf16[8,32]{1,0:T(8,128)(2,1)S(1)}, bf16[8,32]{1,0:T(8,128)(2,1)}, u32[]{:S(2)}) copy-start(bf16[8,32]{1,0:T(8,128)(2,1)} %param.14) | copy-start | bytes 1540
  0.7 14.6 %copy-start.7 = (f32[128]{0:T(128)S(1)}, f32[128]{0:T(128)}, u32[]{:S(2)}) copy-start(f32[128]{0:T(128)} %param.13) | copy-start | bytes 1540
  4.7 41.4 %all-to-all-start = ((bf16[16,592,128]{2,1,0:T(8,128)(2,1)}), bf16[16,592,128]{2,1,0:T(8,128)(2,1)S(1)}, u32[]{:S(2)}, u32[]{:S(2)}) async-start(bf16[16,592,128]{2,1,0:T(8,128)(2,1)} %payload.1), calls=%async_computation | async-start | bytes 4849664 | tf_op jit(solution)/shard_map/all_to_all | solution.py:372
  13.4 1.1 %copy-start.2 = (bf16[2560,256]{1,0:T(8,128)(2,1)}, bf16[2560,256]{1,0:T(8,128)(2,1)S(1)}, u32[]{:S(2)}) copy-start(bf16[2560,256]{1,0:T(8,128)(2,1)S(1)} %get-tuple-element.11.m) | copy-start | bytes 3932164
  14.6 0.7 copy-start.3
  49.5 1.4 %copy-start = (bf16[16,576,128]{2,1,0:T(8,128)(2,1)}, bf16[16,576,128]{2,1,0:T(8,128)(2,1)S(1)}, u32[]{:S(2)}) copy-start(bf16[16,576,128]{2,1,0:T(8,128)(2,1)S(1)} %permute.1) | copy-start | bytes 7077892
  50.9 39.6 %all-to-all-start.1 = ((bf16[16,576,128]{2,1,0:T(8,128)(2,1)}), bf16[16,576,128]{2,1,0:T(8,128)(2,1)}, u32[]{:S(2)}, u32[]{:S(2)}) async-start(bf16[16,576,128]{2,1,0:T(8,128)(2,1)} %copy-done), calls=%async_computation.1 | async-start | bytes 4718592 | tf_op jit(solution)/shard_map/all_to_all | solution.py:383
  58.1 32.4 %copy-start.1 = (f32[18,128,128]{2,1,0:T(8,128)S(1)}, f32[18,128,128]{2,1,0:T(8,128)}, u32[]{:S(2)}) copy-start(f32[18,128,128]{2,1,0:T(8,128)} %broadcast_in_dim.23.w) | copy-start | bytes 3538948

commit v4 on v3

--- a/solution.py
+++ b/solution.py
@@ -14,8 +14,9 @@
 HALF_T = 32
 PAIR_K = 640
 VMEM_LIMIT = 56 * 2**20
-EDGE_VMEM = 52 * 2**20
-FIRST = 6
+EDGE_VMEM = 50 * 2**20
+FIRST = 9
+TABLE_ROWS = 256
 
 
 def params(limit=VMEM_LIMIT):
@@ -26,58 +27,53 @@
     return pl.CostEstimate(flops=flops, bytes_accessed=bytes_accessed, transcendentals=0)
 
 
-def dip_order(dips):
-    return list(range(0, dips, 2)) + list(range(1, dips, 2))
-
-
-def matrices_kernel(taps_x, taps_t, m, xi, xe):
-    dips = taps_x.shape[0]
+def fill_time_bands(taps, m):
     row = lax.broadcasted_iota(jnp.int32, (TILE, TILE), 0)
     col = lax.broadcasted_iota(jnp.int32, (TILE, TILE), 1)
-    for c in range(dips):
-        base = jnp.broadcast_to(taps_t[c : c + 1], (TILE, TILE))
+    for c in range(taps.shape[0]):
+        base = jnp.broadcast_to(taps[c : c + 1], (TILE, TILE))
         band = pltpu.roll(base, 0, 1, stride=1, stride_axis=0)
         at = c * (PAIR_K // 2)
         m[at : at + TILE] = jnp.where(col <= row, band, 0.0).astype(BF16)
         m[at + TILE : at + PAIR_K // 2] = jnp.where(col > row, band, 0.0)[:64].astype(BF16)
-    rows = xi.shape[0] // dips
-    for i, c in enumerate(dip_order(dips)):
-        base = jnp.broadcast_to(taps_x[c : c + 1], (rows, 128))
-        band = pltpu.roll(base, 0, 1, stride=1, stride_axis=0)
-        xi[i * rows : (i + 1) * rows] = band.astype(BF16)
-        xe[i * 32 : i * 32 + 16] = band[:16, :96].astype(BF16)
-        xe[i * 32 + 16 : i * 32 + 32] = band[48:64, :96].astype(BF16)
-
-
-def matrices(dip_trace, dip_time, rows):
+
+
+def trace_bands(taps, rows):
+    dips = taps.shape[0]
+    for c in list(range(0, dips, 2)) + list(range(1, dips, 2)):
+        base = jnp.broadcast_to(taps[c : c + 1], (rows, 128))
+        yield pltpu.roll(base, 0, 1, stride=1, stride_axis=0).astype(BF16)
+
+
+def spread_taps(dip_trace, dip_time):
     dips, taps = dip_time.shape
     taps_x = jnp.pad(dip_trace.astype(F32), ((0, 0), (0, 128 - dip_trace.shape[1])))
     taps_t = dip_time.astype(F32)
     gap = jnp.zeros((dips, TILE - taps), F32)
-    taps_t = jnp.concatenate([taps_t[:, :1], gap, taps_t[:, :0:-1]], axis=1)
-    return pl.pallas_call(
-        matrices_kernel,
-        out_shape=(
-            jax.ShapeDtypeStruct((dips * PAIR_K // 2, TILE), BF16),
-            jax.ShapeDtypeStruct((dips * rows, 128), BF16),
-            jax.ShapeDtypeStruct((dips * 32, 96), BF16),
-        ),
-        compiler_params=pltpu.CompilerParams(vmem_limit_bytes=16 * 2**20),
-        cost_estimate=cost(0, 2**21),
-        name="matrices",
-    )(taps_x, taps_t)
+    return taps_x, jnp.concatenate([taps_t[:, :1], gap, taps_t[:, :0:-1]], axis=1)
+
+
+def turned(x, by):
+    return jnp.concatenate([x[:, x.shape[1] - by :], x[:, : x.shape[1] - by]], axis=1)
 
 
 def time_lhs(tp, dips, rows, tile):
-    base = tile * TILE
-    low = lax.broadcasted_iota(jnp.int32, (rows, 128), 1) < 64
+    samples = tp.shape[1]
+    lane = lax.broadcasted_iota(jnp.int32, (rows, 128), 1)
+    zero = jnp.zeros((rows, 128), BF16)
+    first, last = tile == 0, tile == samples // TILE - 1
+    at = [(tile * TILE + 128 * k) % samples for k in range(3)]
     parts = []
     for pair in range(dips // 2):
-        even = pl.ds(pair * rows, rows)
-        odd = pl.ds((dips // 2 + pair) * rows, rows)
-        parts.append(tp[even, base : base + 256])
-        parts.append(jnp.where(low, tp[even, base + 256 : base + 384], tp[odd, base : base + 128]))
-        parts.append(tp[odd, base + 128 : base + 384])
+        even = [tp[pl.ds(pair * rows, rows), lo : lo + 128] for lo in at]
+        odd = [tp[pl.ds((dips // 2 + pair) * rows, rows), lo : lo + 128] for lo in at]
+        if first:
+            even[0] = jnp.where(lane < HALF_T, zero, even[0])
+            odd[0] = jnp.where(lane < HALF_T + 64, zero, odd[0])
+        if last:
+            even[2] = jnp.where(lane < HALF_T, even[2], zero)
+            odd[2] = jnp.where(lane < HALF_T + 64, odd[2], zero)
+        parts += [even[0], even[1], jnp.where(lane < 64, even[2], odd[0]), odd[1], odd[2]]
     return jnp.concatenate(parts, axis=1)
 
 
@@ -88,24 +84,27 @@
 
 
 def column_tiles(samples):
-    return [(lo, min(lo + TILE, samples + 128)) for lo in range(0, samples + 128, TILE)]
-
-
-def interior_kernel(dips, count, x, w, xi, m, *refs):
-    o, shifted, tp = refs[-3:]
+    return [(lo, lo + TILE) for lo in range(0, samples, TILE)]
+
+
+def interior_kernel(start, count, x, w, taps_x, taps_t, *refs):
+    o, shifted, tp, xi, m = refs[-5:]
+    dips = taps_x.shape[0]
     rows = x.shape[1] - 2 * EDGE
     samples = x.shape[2]
     half = dips // 2 * rows
-    slot = pl.program_id(0) + count[1]
+    slot = pl.program_id(0) + start
 
     @pl.when(pl.program_id(0) == 0)
     def _():
-        shifted[...] = jnp.zeros_like(shifted)
+        fill_time_bands(taps_t, m)
+        for i, band in enumerate(trace_bands(taps_x, rows)):
+            xi[i * rows : (i + 1) * rows] = band
 
     @pl.when(slot < count[0])
     def _():
-        shifted[0, :, HALF_T : HALF_T + samples] = x[0]
-        shifted[1, :, HALF_T + 64 : HALF_T + 64 + samples] = x[0]
+        for k in range(2):
+            shifted[k] = turned(x[0], HALF_T + 64 * k)
         for k in range(2):
             for lo, hi in column_tiles(samples):
                 tp[k * half : (k + 1) * half, lo:hi] = jnp.dot(
@@ -126,33 +125,36 @@
         o[...] = jnp.zeros_like(o)
 
 
-def interior(count, x, w, xi, m, start, steps, out=None):
+def interior(count, x, w, taps_x, taps_t, start, steps, out=None):
     slots, block, samples = x.shape
-    dips = m.shape[0] * 2 // PAIR_K
-    fetch = lambda i, n: (jnp.minimum(i + n[1], jnp.maximum(n[0] - 1, 0)), 0, 0)
+    dips = taps_x.shape[0]
+    inner = dips * (block - 2 * EDGE)
+    fetch = lambda i, n: (jnp.minimum(i + start, jnp.maximum(n[0] - 1, 0)), 0, 0)
     in_specs = [
         pl.BlockSpec((1, block, samples), fetch),
         pl.BlockSpec((1, block, 128), fetch),
-        pl.BlockSpec(xi.shape, lambda i, n: (0, 0)),
-        pl.BlockSpec(m.shape, lambda i, n: (0, 0)),
+        pl.BlockSpec(taps_x.shape, lambda i, n: (0, 0)),
+        pl.BlockSpec(taps_t.shape, lambda i, n: (0, 0)),
     ]
-    args = [jnp.stack([count, jnp.int32(start)]), x, w, xi, m]
+    args = [count, x, w, taps_x, taps_t]
     aliases = {}
     if out is not None:
         in_specs.append(pl.BlockSpec(memory_space=pl.ANY))
         args.append(out)
         aliases = {5: 0}
     return pl.pallas_call(
-        functools.partial(interior_kernel, dips),
+        functools.partial(interior_kernel, start),
         out_shape=jax.ShapeDtypeStruct(x.shape, BF16),
         grid_spec=pltpu.PrefetchScalarGridSpec(
             num_scalar_prefetch=1,
             grid=(steps,),
             in_specs=in_specs,
-            out_specs=pl.BlockSpec((1, block, samples), lambda i, n: (i + n[1], 0, 0)),
+            out_specs=pl.BlockSpec((1, block, samples), lambda i, n: (i + start, 0, 0)),
             scratch_shapes=[
-                pltpu.VMEM((2, block, samples + 128), BF16),
-                pltpu.VMEM((xi.shape[0], samples + 128), BF16),
+                pltpu.VMEM((2, block, samples), BF16),
+                pltpu.VMEM((inner, samples), BF16),
+                pltpu.VMEM((inner, block), BF16),
+                pltpu.VMEM((dips * PAIR_K // 2, TILE), BF16),
             ],
         ),
         input_output_aliases=aliases,
@@ -162,7 +164,10 @@
     )(*args)
 
 
-def edge_kernel(dips, groups, count, xt, xb, halo, w, xe, m, _, o, shifted, tp, res, sems):
+def edge_kernel(
+    groups, count, xt, xb, halo, w, taps_x, taps_t, _, o, shifted, tp, res, xe, m, sems
+):
+    dips = taps_x.shape[0]
     g = pl.program_id(0)
     per = xt.shape[0]
     samples = xt.shape[2]
@@ -186,7 +191,10 @@
 
     @pl.when(g == 0)
     def _():
-        shifted[...] = jnp.zeros_like(shifted)
+        fill_time_bands(taps_t, m)
+        for i, band in enumerate(trace_bands(taps_x, 64)):
+            xe[i * 32 : i * 32 + 16] = band[:16, :96]
+            xe[i * 32 + 16 : i * 32 + 32] = band[48:, :96]
 
     @pl.when(live)
     def _():
@@ -196,11 +204,11 @@
             above = jnp.concatenate(above, axis=1)
             below = jnp.concatenate(below, axis=1)
             for k in range(2):
-                here = slice(HALF_T + 64 * k, HALF_T + 64 * k + samples)
-                shifted[k, i, 0:16, here] = above
-                shifted[k, i, 16:48, here] = xt[i]
-                shifted[k, i, 48:80, here] = xb[i]
-                shifted[k, i, 80:96, here] = below
+                by = HALF_T + 64 * k
+                shifted[k, i, 0:16] = turned(above, by)
+                shifted[k, i, 16:48] = turned(xt[i], by)
+                shifted[k, i, 48:80] = turned(xb[i], by)
+                shifted[k, i, 80:96] = turned(below, by)
                 for lo, hi in column_tiles(samples):
                     part = jnp.dot(
                         xe[k * half : (k + 1) * half],
@@ -236,13 +244,13 @@
                     copy.wait()
 
 
-def edges(count, x, halo, w, xe, m, out, per=6):
+def edges(count, x, halo, w, taps_x, taps_t, out, per=6):
     slots, block, samples = x.shape
-    dips = m.shape[0] * 2 // PAIR_K
+    dips = taps_x.shape[0]
     groups = slots // per
     last = lambda g, n: jnp.minimum(g, jnp.maximum(n[0] - 1, 0) // per)
     return pl.pallas_call(
-        functools.partial(edge_kernel, dips, groups),
+        functools.partial(edge_kernel, groups),
         out_shape=jax.ShapeDtypeStruct(x.shape, BF16),
         grid_spec=pltpu.PrefetchScalarGridSpec(
             num_scalar_prefetch=1,
@@ -252,15 +260,17 @@
                 pl.BlockSpec((per, 32, samples), lambda g, n: (last(g, n), 3, 0)),
                 pl.BlockSpec((halo.shape[0], per * 32, 128), lambda g, n: (0, last(g, n), 0)),
                 pl.BlockSpec((per, block, 128), lambda g, n: (last(g, n), 0, 0)),
-                pl.BlockSpec(xe.shape, lambda g, n: (0, 0)),
-                pl.BlockSpec(m.shape, lambda g, n: (0, 0)),
+                pl.BlockSpec(taps_x.shape, lambda g, n: (0, 0)),
+                pl.BlockSpec(taps_t.shape, lambda g, n: (0, 0)),
                 pl.BlockSpec(memory_space=pl.ANY),
             ],
             out_specs=pl.BlockSpec(memory_space=pl.ANY),
             scratch_shapes=[
-                pltpu.VMEM((2, per, 96, samples + 128), BF16),
-                pltpu.VMEM((dips * per * 32, samples + 128), BF16),
+                pltpu.VMEM((2, per, 96, samples), BF16),
+                pltpu.VMEM((dips * per * 32, samples), BF16),
                 pltpu.VMEM((groups, per, 32, samples), BF16),
+                pltpu.VMEM((dips * 32, 96), BF16),
+                pltpu.VMEM((dips * PAIR_K // 2, TILE), BF16),
                 pltpu.SemaphoreType.DMA((groups, 2)),
             ],
         ),
@@ -268,7 +278,7 @@
         compiler_params=params(EDGE_VMEM),
         cost_estimate=cost(8_000_000_000, 2**23),
         name="edges",
-    )(count.reshape(1), x, x, halo, w, xe, m, out)
+    )(count, x, x, halo, w, taps_x, taps_t, out)
 
 
 def payload_kernel(per_line, count, dest, offset, xt, xb, o):
@@ -366,23 +376,25 @@
 ):
     x = shot_traces[0]
     slots, block, samples = x.shape
-    count = block_count[0, 0]
+    count = block_count.reshape(1)
 
     ends = payload(block_count, slot_dest, slot_offset, x)
     ends = lax.all_to_all(ends, "rline", split_axis=0, concat_axis=0, tiled=True)
 
-    amps = lax.all_gather(amp_table, "shot", axis=0, tiled=True)
+    wide = jnp.broadcast_to(amp_table, (TABLE_ROWS, amp_table.shape[0]))
+    wide = lax.all_gather(lax.optimization_barrier(wide), "shot", axis=0, tiled=False)
+    amps = lax.optimization_barrier(wide)[:, 0].reshape(-1)
     table_hit = amp_index[0][:, :, None] == jnp.arange(amps.shape[0], dtype=jnp.int32)
     weight = jnp.sum(jnp.where(table_hit, amps, F32(0.0)), axis=2)
     weight = jnp.broadcast_to(weight[:, :, None], (slots, block, 128))
-    m, xi, xe = matrices(dip_trace, dip_time, block - 2 * EDGE)
-
-    out = interior(count, x, weight, xi, m, 0, FIRST)
+    taps_x, taps_t = spread_taps(dip_trace, dip_time)
+
+    out = interior(count, x, weight, taps_x, taps_t, 0, FIRST)
     ends, out = lax.optimization_barrier((ends, out))
     moved = permute(ends, slots)
     halo = lax.all_to_all(moved, "rline", split_axis=0, concat_axis=0, tiled=True)
-    out = interior(count, x, weight, xi, m, FIRST, slots - FIRST, out)
-    out = edges(count, x, halo, weight, xe, m, out)
+    out = interior(count, x, weight, taps_x, taps_t, FIRST, slots - FIRST, out)
+    out = edges(count, x, halo, weight, taps_x, taps_t, out)
     return out[None]
 
 

time: 107 us -> 126 us (1.18)
  waiting for transfers between devices: 2.77 us -> 28.5 us
  between operations: 0.74 us -> 14.1 us
  blocking collectives: 10.5 us -> 0 us
  Pallas kernels: 69.1 us -> 60.2 us
    all_to_all x1, waiting for transfers between devices: 2.77 us -> 16.2 us  [shards(): lax.all_to_all(moved, 'rline', split_axis=0, concat_axis=0, tiled=True)]
    all_gather x0 -> x1, waiting for transfers between devices: none -> 12.3 us  [shards(): lax.all_gather(lax.optimization_barrier(wide), 'shot', axis=0, tiled=False)]
    all_gather x1 -> x0, blocking collectives: 10.5 us -> none  [shards(): amps = lax.all_gather(amp_table, 'shot', axis=0, tiled=True)]
    pallas_call x4 -> x3, Pallas kernels: 61.7 us -> 52.8 us  [the longest x2 37.6 us: interior(): pl.pallas_call(functools.partial(interior_kernel, start), out_shape=jax.S...]
    unnamed x17 -> x15, local copies, waits for them, and re-layouts: 3.21 us -> 1.43 us
    broadcast_in_dim x1 -> x2, local copies, waits for them, and re-layouts: 0.01 us -> 1.32 us  [the longest x1 1.32 us: shards(): wide = jnp.broadcast_to(amp_table, (TABLE_ROWS, amp_table.shape[0]))]
    another operation x2 -> x0, other arithmetic: 1.31 us -> none  [interior(): args = [jnp.stack([count, jnp.int32(start)]), x, w, xi, m]]
  transfers between devices with their start and end apart: 2 -> 3, of which waited for: 1 -> 2; matrix products, arithmetic and copies ran while one was open for 4% -> 4% of each run, Pallas kernels for 44% -> 33%
where the time goes in v4:
time: 126 us
  Pallas kernels  60.2 us (48%)
  waiting for transfers between devices  28.5 us (23%)
  starting transfers between devices  15.4 us (12%)
  between operations  14.1 us (11%)
  local copies, waits for them, and re-layouts  5.14 us (4%)
  other arithmetic  2.7 us (2%)
    pallas_call x2, Pallas kernels, interior(): pl.pallas_call(functools.partial(interior_kernel, start), out_shape=jax.S...  37.6 us
    all_to_all x1, waiting for transfers between devices, shards(): lax.all_to_all(moved, 'rline', split_axis=0, concat_axis=0, tiled=True)  16.2 us
    pallas_call x1, Pallas kernels, edges(): pl.pallas_call(functools.partial(edge_kernel, groups), out_shape=jax.Shap...  15.2 us
    all_gather x1, waiting for transfers between devices, shards(): lax.all_gather(lax.optimization_barrier(wide), 'shot', axis=0, tiled=False)  12.3 us
    all_to_all x1, starting transfers between devices, shards(): lax.all_to_all(ends, 'rline', split_axis=0, concat_axis=0, tiled=True)  8.06 us
    all_to_all x1, starting transfers between devices, shards(): lax.all_to_all(moved, 'rline', split_axis=0, concat_axis=0, tiled=True)  7.31 us
    pallas_call x1, Pallas kernels, payload(): pl.pallas_call(functools.partial(payload_kernel, slots // 2), out_shape=j...  4.05 us
    pallas_call x1, Pallas kernels, permute(): pl.pallas_call(functools.partial(permute_kernel, slots), out_shape=jax.Sh...  3.32 us
  transfers between devices with their start and end apart: 3, of which 2 were waited for; matrix products, arithmetic and copies ran while one was open for 4% of the time, Pallas kernels for 33%

profile of v4, /device:TPU:32, one launch (start us, length us, event | category | flops | bytes accessed | tf_op | source)
XLA Modules:
  0.0 126.0 jit_solution(10068571677710212593)
XLA Ops:
  6.5 0.0 all-gather.3.cloned.1.call-start
  6.5 1.3 %broadcast_in_dim.24 = f32[256,128]{1,0:T(8,128)} broadcast(f32[128]{0:T(128)} %param.13), dimensions={1} | broadcast | bytes 131584 | tf_op jit(solution)/shard_map/broadcast_in_dim | solution.py:384
  7.9 0.0 all-gather.3.cloned.1.call-update
  8.5 0.0 copy-start.6
  8.5 0.0 copy-start.4
  8.6 0.0 copy-start.5
  8.6 4.1 %payload.1 = bf16[16,592,128]{2,1,0:T(8,128)(2,1)} custom-call(s32[1,1]{1,0:T(1,128)} %copy.16.count, s32[1,18]{1,0:T(1,128)} %dest.1, s32[1,18]{1,0:T(1,128)} %offset.1, bf16[18,128,2048]{2,1,0:T(8,128)(2,1)} %bitcast.13, bf16[18,128,2048]{2,1,0:T(8,128)(2,1)} %bitcast.14), custom_call_target="tpu_custom_call" | custom-call | bytes 4194304 | tf_op jit(solution)/shard_map/payload/pallas_call | solution.py:301
  12.6 8.1 %all-to-all-start = ((bf16[16,592,128]{2,1,0:T(8,128)(2,1)}), bf16[16,592,128]{2,1,0:T(8,128)(2,1)S(1)}, u32[]{:S(2)}, u32[]{:S(2)}) async-start(bf16[16,592,128]{2,1,0:T(8,128)(2,1)} %payload.1), calls=%async_computation | async-start | bytes 4849664 | tf_op jit(solution)/shard_map/all_to_all | solution.py:382
  20.7 0.0 copy-done.6
  20.7 0.6 pad_convert_fusion.taps_x
  21.3 0.0 copy-done.4
  21.3 0.1 slice.11
  21.4 0.1 rev.3
  21.4 0.0 copy-done.5
  21.4 0.1 pad.9.clone
  21.5 0.7 pad_maximum_fusion.taps_t
  22.2 12.3 %all-gather.3.cloned.1.call-done = f32[2048,128]{1,0:T(8,128)} async-done(((f32[256,128]{1,0:T(8,128)}), f32[2048,128]{1,0:T(8,128)}) %all-gather.3.cloned.1.call-update) | async-done | bytes 1048592 | tf_op jit(solution)/shard_map/all_gather | solution.py:385
  34.5 0.8 slice.12
  35.2 1.4 %select_reduce_fusion = f32[18,128]{1,0:T(8,128)S(1)} fusion(f32[1024]{0:T(1024)S(1)} %bitcast.20, s32[18,128]{1,0:T(8,128)S(1)} %bitcast.19), kind=kLoop, calls=%fused_computation | loop fusion | flops 7075584 | bytes 22528 | tf_op jit(solution)/shard_map/reduce_sum | solution.py:388
  36.7 1.4 %broadcast_in_dim.27.w = f32[18,128,128]{2,1,0:T(8,128)} broadcast(f32[18,128]{1,0:T(8,128)S(1)} %select_reduce_fusion), dimensions={0,1} | broadcast | bytes 1188864 | tf_op jit(solution)/shard_map/broadcast_in_dim | solution.py:389
  38.1 21.5 %interior.2.refs_0_ = bf16[18,128,2048]{2,1,0:T(8,128)(2,1)} custom-call(s32[1]{0:T(128)} %bitcast.9.count, bf16[18,128,2048]{2,1,0:T(8,128)(2,1)} %bitcast.15, f32[18,128,128]{2,1,0:T(8,128)} %broadcast_in_dim.27.w, f32[8,128]{1,0:T(8,128)} %pad_convert_fusion.taps_x, f32[8,256]{1,0:T(8,128)} %pad_maximum_fusion.taps_t), custom_call_target="tpu_custom_call" | custom-call | flops 17999998976 | bytes 9437184 | tf_op jit(solution)/shard_map/interior/pallas_call | solution.py:145
  59.6 0.0 all-to-all-done
  59.6 3.3 %permute.1 = bf16[16,576,128]{2,1,0:T(8,128)(2,1)S(1)} custom-call(bf16[9472,128]{1,0:T(8,128)(2,1)S(1)} %bitcast.12), custom_call_target="tpu_custom_call" | custom-call | bytes 8388608 | tf_op jit(solution)/shard_map/permute/pallas_call | solution.py:357
  62.9 0.0 copy-start
  62.9 1.4 %copy-done = bf16[16,576,128]{2,1,0:T(8,128)(2,1)} copy-done((bf16[16,576,128]{2,1,0:T(8,128)(2,1)}, bf16[16,576,128]{2,1,0:T(8,128)(2,1)S(1)}, u32[]{:S(2)}) %copy-start) | copy-done | bytes 2359320
  64.3 7.3 %all-to-all-start.1 = ((bf16[16,576,128]{2,1,0:T(8,128)(2,1)}), bf16[16,576,128]{2,1,0:T(8,128)(2,1)S(1)}, u32[]{:S(2)}, u32[]{:S(2)}) async-start(bf16[16,576,128]{2,1,0:T(8,128)(2,1)} %copy-done), calls=%async_computation.1 | async-start | bytes 4718592 | tf_op jit(solution)/shard_map/all_to_all | solution.py:395
  71.6 0.0 copy-start.2
  71.6 0.0 copy-start.3
  71.6 16.2 %interior.3._ = bf16[18,128,2048]{2,1,0:T(8,128)(2,1)} custom-call(s32[1]{0:T(128)} %bitcast.10.count, bf16[18,128,2048]{2,1,0:T(8,128)(2,1)} %bitcast.16, f32[18,128,128]{2,1,0:T(8,128)} %broadcast_in_dim.27.w, f32[8,128]{1,0:T(8,128)} %pad_convert_fusion.taps_x, f32[8,256]{1,0:T(8,128)} %pad_maximum_fusion.taps_t, ...), custom_call_target="tpu_custom_call", output_to_operand_aliasing={{}: (5, {})} | custom-call | flops 17999998976 | bytes 9437184 | tf_op jit(solution)/shard_map/interior/pallas_call | solution.py:145
  87.8 16.2 %all-to-all-done.1.halo = bf16[16,576,128]{2,1,0:T(8,128)(2,1)S(1)} async-done(((bf16[16,576,128]{2,1,0:T(8,128)(2,1)}), bf16[16,576,128]{2,1,0:T(8,128)(2,1)S(1)}, u32[]{:S(2)}, u32[]{:S(2)}) %all-to-all-start.1) | async-done | bytes 2359328 | tf_op jit(solution)/shard_map/all_to_all | solution.py:395
  104.0 0.0 copy-done.2
  104.0 15.2 %edges.1 = bf16[18,128,2048]{2,1,0:T(8,128)(2,1)} custom-call(s32[1]{0:T(128)} %bitcast.11.count, bf16[18,128,2048]{2,1,0:T(8,128)(2,1)} %bitcast.17, bf16[18,128,2048]{2,1,0:T(8,128)(2,1)} %bitcast.18, bf16[16,576,128]{2,1,0:T(8,128)(2,1)S(1)} %all-to-all-done.1.halo, f32[18,128,128]{2,1,0:T(8,128)S(1)} %copy-done.1, ...), custom_call_target="tpu_custom_call", output_to_operand_aliasing={{}: (7, {})} | custom-call | flops 8000000000 | bytes 8388608 | tf_op jit(solution)/shard_map/edges/pallas_call | solution.py:252
  (6 shorter events, 0.0 us)
Async XLA Ops:
  6.5 28.0 %all-gather.3.cloned.1.call-start = ((), (), s32[]{:S(2)}) async-start(), calls=%async_computation.2 | async-start | bytes 1179648 | tf_op jit(solution)/shard_map/all_gather | solution.py:385
  8.5 12.2 %copy-start.6 = (bf16[8,32]{1,0:T(8,128)(2,1)S(1)}, bf16[8,32]{1,0:T(8,128)(2,1)}, u32[]{:S(2)}) copy-start(bf16[8,32]{1,0:T(8,128)(2,1)} %param.14) | copy-start | bytes 1540
  8.5 12.7 %copy-start.4 = (bf16[8,64]{1,0:T(8,128)(2,1)S(1)}, bf16[8,64]{1,0:T(8,128)(2,1)}, u32[]{:S(2)}) copy-start(bf16[8,64]{1,0:T(8,128)(2,1)} %param.15) | copy-start | bytes 3076
  8.6 12.9 %copy-start.5 = (s32[1,18,128]{2,0,1:T(1,128)S(1)}, s32[1,18,128]{2,0,1:T(1,128)}, u32[]{:S(2)}) copy-start(s32[1,18,128]{2,0,1:T(1,128)} %param.12) | copy-start | bytes 27652
  12.6 46.9 %all-to-all-start = ((bf16[16,592,128]{2,1,0:T(8,128)(2,1)}), bf16[16,592,128]{2,1,0:T(8,128)(2,1)S(1)}, u32[]{:S(2)}, u32[]{:S(2)}) async-start(bf16[16,592,128]{2,1,0:T(8,128)(2,1)} %payload.1), calls=%async_computation | async-start | bytes 4849664 | tf_op jit(solution)/shard_map/all_to_all | solution.py:382
  62.9 1.4 %copy-start = (bf16[16,576,128]{2,1,0:T(8,128)(2,1)}, bf16[16,576,128]{2,1,0:T(8,128)(2,1)S(1)}, u32[]{:S(2)}) copy-start(bf16[16,576,128]{2,1,0:T(8,128)(2,1)S(1)} %permute.1) | copy-start | bytes 7077892
  64.3 39.7 %all-to-all-start.1 = ((bf16[16,576,128]{2,1,0:T(8,128)(2,1)}), bf16[16,576,128]{2,1,0:T(8,128)(2,1)S(1)}, u32[]{:S(2)}, u32[]{:S(2)}) async-start(bf16[16,576,128]{2,1,0:T(8,128)(2,1)} %copy-done), calls=%async_computation.1 | async-start | bytes 4718592 | tf_op jit(solution)/shard_map/all_to_all | solution.py:395
  71.6 32.4 %copy-start.1 = (f32[18,128,128]{2,1,0:T(8,128)S(1)}, f32[18,128,128]{2,1,0:T(8,128)}, u32[]{:S(2)}) copy-start(f32[18,128,128]{2,1,0:T(8,128)} %broadcast_in_dim.27.w) | copy-start | bytes 3538948
  71.6 32.4 %copy-start.2 = (f32[8,256]{1,0:T(8,128)S(1)}, f32[8,256]{1,0:T(8,128)}, u32[]{:S(2)}) copy-start(f32[8,256]{1,0:T(8,128)} %pad_maximum_fusion.taps_t) | copy-start | bytes 24580
  71.6 32.4 %copy-start.3 = (f32[8,128]{1,0:T(8,128)S(1)}, f32[8,128]{1,0:T(8,128)}, u32[]{:S(2)}) copy-start(f32[8,128]{1,0:T(8,128)} %pad_convert_fusion.taps_x) | copy-start | bytes 12292
Sparse Core Ops, SparseCore 0:
  9.1 25.3 all-gather.2

commit v5 on v4

--- a/solution.py
+++ b/solution.py
@@ -15,8 +15,7 @@
 PAIR_K = 640
 VMEM_LIMIT = 56 * 2**20
 EDGE_VMEM = 50 * 2**20
-FIRST = 9
-TABLE_ROWS = 256
+FIRST = 6
 
 
 def params(limit=VMEM_LIMIT):
@@ -381,9 +380,7 @@
     ends = payload(block_count, slot_dest, slot_offset, x)
     ends = lax.all_to_all(ends, "rline", split_axis=0, concat_axis=0, tiled=True)
 
-    wide = jnp.broadcast_to(amp_table, (TABLE_ROWS, amp_table.shape[0]))
-    wide = lax.all_gather(lax.optimization_barrier(wide), "shot", axis=0, tiled=False)
-    amps = lax.optimization_barrier(wide)[:, 0].reshape(-1)
+    amps = lax.all_gather(amp_table, "shot", axis=0, tiled=True)
     table_hit = amp_index[0][:, :, None] == jnp.arange(amps.shape[0], dtype=jnp.int32)
     weight = jnp.sum(jnp.where(table_hit, amps, F32(0.0)), axis=2)
     weight = jnp.broadcast_to(weight[:, :, None], (slots, block, 128))

time: 126 us -> 104 us (0.83)
  the two profiles are of different devices: /device:TPU:32 before, /device:TPU:0 now
where the time goes in v5:
time: 104 us; the launch traced here: 103 us
  Pallas kernels  60.1 us (58%)
  waiting for transfers between devices  13.9 us (13%)
  starting transfers between devices  11.9 us (11%)
  blocking collectives  10.5 us (10%)
  local copies, waits for them, and re-layouts  3.07 us (3%)
  other arithmetic  2.7 us (3%)
    pallas_call x2, Pallas kernels, interior(): pl.pallas_call(functools.partial(interior_kernel, start), out_shape=jax.S...  37.6 us
    pallas_call x1, Pallas kernels, edges(): pl.pallas_call(functools.partial(edge_kernel, groups), out_shape=jax.Shap...  15.2 us
    all_gather x1, blocking collectives, shards(): amps = lax.all_gather(amp_table, 'shot', axis=0, tiled=True)  10.5 us
    all_to_all x1, waiting for transfers between devices, shards(): lax.all_to_all(moved, 'rline', split_axis=0, concat_axis=0, tiled=True)  9.23 us
    all_to_all x1, starting transfers between devices, shards(): lax.all_to_all(ends, 'rline', split_axis=0, concat_axis=0, tiled=True)  8.13 us
    all_to_all x1, waiting for transfers between devices, shards(): lax.all_to_all(ends, 'rline', split_axis=0, concat_axis=0, tiled=True)  4.65 us
    pallas_call x1, Pallas kernels, payload(): pl.pallas_call(functools.partial(payload_kernel, slots // 2), out_shape=j...  4.03 us
    all_to_all x1, starting transfers between devices, shards(): lax.all_to_all(moved, 'rline', split_axis=0, concat_axis=0, tiled=True)  3.72 us
  transfers between devices with their start and end apart: 2, of which 2 were waited for; matrix products, arithmetic and copies ran while one was open for 4% of the time, Pallas kernels for 37%

profile of v5, /device:TPU:0, one launch (start us, length us, event | category | flops | bytes accessed | tf_op | source)
XLA Modules:
  0.0 102.9 jit_solution(14793208117286157366)
XLA Ops:
  0.7 0.0 copy-start.4
  0.7 0.0 copy-start.5
  0.7 0.0 copy-start.7
  0.7 0.0 copy-start.6
  0.7 4.0 %payload.1 = bf16[16,592,128]{2,1,0:T(8,128)(2,1)} custom-call(s32[1,1]{1,0:T(1,128)} %copy.16.count, s32[1,18]{1,0:T(1,128)} %dest.1, s32[1,18]{1,0:T(1,128)} %offset.1, bf16[18,128,2048]{2,1,0:T(8,128)(2,1)} %bitcast.13, bf16[18,128,2048]{2,1,0:T(8,128)(2,1)} %bitcast.14), custom_call_target="tpu_custom_call" | custom-call | bytes 4194304 | tf_op jit(solution)/shard_map/payload/pallas_call | solution.py:300
  4.7 8.1 %all-to-all-start = ((bf16[16,592,128]{2,1,0:T(8,128)(2,1)}), bf16[16,592,128]{2,1,0:T(8,128)(2,1)S(1)}, u32[]{:S(2)}, u32[]{:S(2)}) async-start(bf16[16,592,128]{2,1,0:T(8,128)(2,1)} %payload.1), calls=%async_computation | async-start | bytes 4849664 | tf_op jit(solution)/shard_map/all_to_all | solution.py:381
  12.9 0.0 copy-done.4
  12.9 0.1 slice.7
  13.0 0.1 rev.3
  13.0 0.0 copy-done.5
  13.0 0.1 pad.9.clone
  13.1 0.0 copy-done.7
  13.1 10.5 %all-gather = f32[8,1,128]{2,1,0:T(1,128)S(1)} all-gather(f32[1,1,128]{2,1,0:T(1,128)S(1)} %bitcast.21), channel_id=1, replica_groups=mesh['shot'=8,'rline'=16] {'shot'}, dimensions={0}, use_global_device_ids=true | all-gather | bytes 4608 | tf_op jit(solution)/shard_map/all_gather | solution.py:383
  23.6 0.0 copy-done.6
  23.6 0.6 pad_convert_fusion.taps_x
  24.2 0.7 pad_maximum_fusion.taps_t
  24.9 1.4 %select_reduce_fusion = f32[18,128]{1,0:T(8,128)S(1)} fusion(f32[1024]{0:T(1024)S(1)} %bitcast.20, s32[18,128]{1,0:T(8,128)S(1)} %bitcast.19), kind=kLoop, calls=%fused_computation | loop fusion | flops 7075584 | bytes 22528 | tf_op jit(solution)/shard_map/reduce_sum | solution.py:385
  26.3 1.4 %broadcast_in_dim.23.w = f32[18,128,128]{2,1,0:T(8,128)} broadcast(f32[18,128]{1,0:T(8,128)S(1)} %select_reduce_fusion), dimensions={0,1} | broadcast | bytes 1188864 | tf_op jit(solution)/shard_map/broadcast_in_dim | solution.py:386
  27.7 15.0 %interior.2.refs_0_ = bf16[18,128,2048]{2,1,0:T(8,128)(2,1)} custom-call(s32[1]{0:T(128)} %bitcast.9.count, bf16[18,128,2048]{2,1,0:T(8,128)(2,1)} %bitcast.15, f32[18,128,128]{2,1,0:T(8,128)} %broadcast_in_dim.23.w, f32[8,128]{1,0:T(8,128)} %pad_convert_fusion.taps_x, f32[8,256]{1,0:T(8,128)} %pad_maximum_fusion.taps_t), custom_call_target="tpu_custom_call" | custom-call | flops 12000000000 | bytes 6291456 | tf_op jit(solution)/shard_map/interior/pallas_call | solution.py:144
  42.7 4.7 %all-to-all-done = bf16[16,592,128]{2,1,0:T(8,128)(2,1)S(1)} async-done(((bf16[16,592,128]{2,1,0:T(8,128)(2,1)}), bf16[16,592,128]{2,1,0:T(8,128)(2,1)S(1)}, u32[]{:S(2)}, u32[]{:S(2)}) %all-to-all-start) | async-done | bytes 2424864 | tf_op jit(solution)/shard_map/all_to_all | solution.py:381
  47.4 3.3 %permute.1 = bf16[16,576,128]{2,1,0:T(8,128)(2,1)S(1)} custom-call(bf16[9472,128]{1,0:T(8,128)(2,1)S(1)} %bitcast.12), custom_call_target="tpu_custom_call" | custom-call | bytes 8388608 | tf_op jit(solution)/shard_map/permute/pallas_call | solution.py:356
  50.7 0.0 copy-start
  50.7 1.4 %copy-done = bf16[16,576,128]{2,1,0:T(8,128)(2,1)} copy-done((bf16[16,576,128]{2,1,0:T(8,128)(2,1)}, bf16[16,576,128]{2,1,0:T(8,128)(2,1)S(1)}, u32[]{:S(2)}) %copy-start) | copy-done | bytes 2359320
  52.1 3.7 %all-to-all-start.1 = ((bf16[16,576,128]{2,1,0:T(8,128)(2,1)}), bf16[16,576,128]{2,1,0:T(8,128)(2,1)S(1)}, u32[]{:S(2)}, u32[]{:S(2)}) async-start(bf16[16,576,128]{2,1,0:T(8,128)(2,1)} %copy-done), calls=%async_computation.1 | async-start | bytes 4718592 | tf_op jit(solution)/shard_map/all_to_all | solution.py:392
  55.8 0.0 copy-start.1
  55.9 0.0 copy-start.2
  55.9 0.0 copy-start.3
  55.9 22.6 %interior.3._ = bf16[18,128,2048]{2,1,0:T(8,128)(2,1)} custom-call(s32[1]{0:T(128)} %bitcast.10.count, bf16[18,128,2048]{2,1,0:T(8,128)(2,1)} %bitcast.16, f32[18,128,128]{2,1,0:T(8,128)} %broadcast_in_dim.23.w, f32[8,128]{1,0:T(8,128)} %pad_convert_fusion.taps_x, f32[8,256]{1,0:T(8,128)} %pad_maximum_fusion.taps_t, ...), custom_call_target="tpu_custom_call", output_to_operand_aliasing={{}: (5, {})} | custom-call | flops 24000000000 | bytes 12582912 | tf_op jit(solution)/shard_map/interior/pallas_call | solution.py:144
  78.5 9.2 %all-to-all-done.1.halo = bf16[16,576,128]{2,1,0:T(8,128)(2,1)S(1)} async-done(((bf16[16,576,128]{2,1,0:T(8,128)(2,1)}), bf16[16,576,128]{2,1,0:T(8,128)(2,1)S(1)}, u32[]{:S(2)}, u32[]{:S(2)}) %all-to-all-start.1) | async-done | bytes 2359328 | tf_op jit(solution)/shard_map/all_to_all | solution.py:392
  87.7 0.0 copy-done.1
  87.7 0.0 copy-done.3
  87.7 15.2 %edges.1 = bf16[18,128,2048]{2,1,0:T(8,128)(2,1)} custom-call(s32[1]{0:T(128)} %bitcast.11.count, bf16[18,128,2048]{2,1,0:T(8,128)(2,1)} %bitcast.17, bf16[18,128,2048]{2,1,0:T(8,128)(2,1)} %bitcast.18, bf16[16,576,128]{2,1,0:T(8,128)(2,1)S(1)} %all-to-all-done.1.halo, f32[18,128,128]{2,1,0:T(8,128)S(1)} %copy-done.1, ...), custom_call_target="tpu_custom_call", output_to_operand_aliasing={{}: (7, {})} | custom-call | flops 8000000000 | bytes 8388608 | tf_op jit(solution)/shard_map/edges/pallas_call | solution.py:251
  (4 shorter events, 0.0 us)
Async XLA Ops:
  0.7 12.2 %copy-start.4 = (bf16[8,64]{1,0:T(8,128)(2,1)S(1)}, bf16[8,64]{1,0:T(8,128)(2,1)}, u32[]{:S(2)}) copy-start(bf16[8,64]{1,0:T(8,128)(2,1)} %param.15) | copy-start | bytes 3076
  0.7 12.4 %copy-start.5 = (s32[1,18,128]{2,0,1:T(1,128)S(1)}, s32[1,18,128]{2,0,1:T(1,128)}, u32[]{:S(2)}) copy-start(s32[1,18,128]{2,0,1:T(1,128)} %param.12) | copy-start | bytes 27652
  0.7 12.4 %copy-start.7 = (f32[128]{0:T(128)S(1)}, f32[128]{0:T(128)}, u32[]{:S(2)}) copy-start(f32[128]{0:T(128)} %param.13) | copy-start | bytes 1540
  0.7 22.9 %copy-start.6 = (bf16[8,32]{1,0:T(8,128)(2,1)S(1)}, bf16[8,32]{1,0:T(8,128)(2,1)}, u32[]{:S(2)}) copy-start(bf16[8,32]{1,0:T(8,128)(2,1)} %param.14) | copy-start | bytes 1540
  4.7 42.6 %all-to-all-start = ((bf16[16,592,128]{2,1,0:T(8,128)(2,1)}), bf16[16,592,128]{2,1,0:T(8,128)(2,1)S(1)}, u32[]{:S(2)}, u32[]{:S(2)}) async-start(bf16[16,592,128]{2,1,0:T(8,128)(2,1)} %payload.1), calls=%async_computation | async-start | bytes 4849664 | tf_op jit(solution)/shard_map/all_to_all | solution.py:381
  50.7 1.4 %copy-start = (bf16[16,576,128]{2,1,0:T(8,128)(2,1)}, bf16[16,576,128]{2,1,0:T(8,128)(2,1)S(1)}, u32[]{:S(2)}) copy-start(bf16[16,576,128]{2,1,0:T(8,128)(2,1)S(1)} %permute.1) | copy-start | bytes 7077892
  52.1 35.6 %all-to-all-start.1 = ((bf16[16,576,128]{2,1,0:T(8,128)(2,1)}), bf16[16,576,128]{2,1,0:T(8,128)(2,1)S(1)}, u32[]{:S(2)}, u32[]{:S(2)}) async-start(bf16[16,576,128]{2,1,0:T(8,128)(2,1)} %copy-done), calls=%async_computation.1 | async-start | bytes 4718592 | tf_op jit(solution)/shard_map/all_to_all | solution.py:392
  55.8 31.9 %copy-start.1 = (f32[18,128,128]{2,1,0:T(8,128)S(1)}, f32[18,128,128]{2,1,0:T(8,128)}, u32[]{:S(2)}) copy-start(f32[18,128,128]{2,1,0:T(8,128)} %broadcast_in_dim.23.w) | copy-start | bytes 3538948
  55.9 31.9 %copy-start.2 = (f32[8,256]{1,0:T(8,128)S(1)}, f32[8,256]{1,0:T(8,128)}, u32[]{:S(2)}) copy-start(f32[8,256]{1,0:T(8,128)} %pad_maximum_fusion.taps_t) | copy-start | bytes 24580
  55.9 31.9 %copy-start.3 = (f32[8,128]{1,0:T(8,128)S(1)}, f32[8,128]{1,0:T(8,128)}, u32[]{:S(2)}) copy-start(f32[8,128]{1,0:T(8,128)} %pad_convert_fusion.taps_x) | copy-start | bytes 12292

commit v6 on v5

--- a/solution.py
+++ b/solution.py
@@ -15,7 +15,7 @@
 PAIR_K = 640
 VMEM_LIMIT = 56 * 2**20
 EDGE_VMEM = 50 * 2**20
-FIRST = 6
+FIRST = 8
 
 
 def params(limit=VMEM_LIMIT):
@@ -29,6 +29,7 @@
 def fill_time_bands(taps, m):
     row = lax.broadcasted_iota(jnp.int32, (TILE, TILE), 0)
     col = lax.broadcasted_iota(jnp.int32, (TILE, TILE), 1)
+    taps = moved_taps(taps[...], TILE, -1)
     for c in range(taps.shape[0]):
         base = jnp.broadcast_to(taps[c : c + 1], (TILE, TILE))
         band = pltpu.roll(base, 0, 1, stride=1, stride_axis=0)
@@ -39,17 +40,21 @@
 
 def trace_bands(taps, rows):
     dips = taps.shape[0]
+    taps = moved_taps(taps[...], 128, 1)
     for c in list(range(0, dips, 2)) + list(range(1, dips, 2)):
         base = jnp.broadcast_to(taps[c : c + 1], (rows, 128))
         yield pltpu.roll(base, 0, 1, stride=1, stride_axis=0).astype(BF16)
 
 
-def spread_taps(dip_trace, dip_time):
-    dips, taps = dip_time.shape
-    taps_x = jnp.pad(dip_trace.astype(F32), ((0, 0), (0, 128 - dip_trace.shape[1])))
-    taps_t = dip_time.astype(F32)
-    gap = jnp.zeros((dips, TILE - taps), F32)
-    return taps_x, jnp.concatenate([taps_t[:, :1], gap, taps_t[:, :0:-1]], axis=1)
+def moved_taps(taps, width, sign):
+    row = lax.broadcasted_iota(jnp.int32, (taps.shape[1], width), 0)
+    col = lax.broadcasted_iota(jnp.int32, (taps.shape[1], width), 1)
+    hit = (col == row) if sign > 0 else ((col == 0) & (row == 0)) | (col + row == width)
+    return jnp.dot(taps, hit.astype(F32).astype(BF16), preferred_element_type=F32)
+
+
+def columns(weight):
+    return jnp.broadcast_to(weight, (weight.shape[1], weight.shape[1])).T
 
 
 def turned(x, by):
@@ -111,7 +116,7 @@
                     shifted[k, :, lo:hi],
                     preferred_element_type=F32,
                 ).astype(BF16)
-        weight = jnp.concatenate([w[0, EDGE : EDGE + rows]] * 2, axis=1)
+        weight = jnp.concatenate([columns(w[0])[EDGE : EDGE + rows]] * 2, axis=1)
         for first in range(0, samples // TILE, 2):
             tiles = (first, first + 1)
             for tile, noise in zip(tiles, noise_tiles(tp, m, dips, rows, tiles)):
@@ -131,7 +136,7 @@
     fetch = lambda i, n: (jnp.minimum(i + start, jnp.maximum(n[0] - 1, 0)), 0, 0)
     in_specs = [
         pl.BlockSpec((1, block, samples), fetch),
-        pl.BlockSpec((1, block, 128), fetch),
+        pl.BlockSpec((1, 1, block), fetch),
         pl.BlockSpec(taps_x.shape, lambda i, n: (0, 0)),
         pl.BlockSpec(taps_t.shape, lambda i, n: (0, 0)),
     ]
@@ -217,6 +222,9 @@
                     for c in range(dips // 2):
                         at = (k * dips // 2 + c) * rows + i * 32
                         tp[at : at + 32, lo:hi] = part[c * 32 : c * 32 + 32]
+        weights = [columns(w[i]) for i in range(per)]
+        tops = [jnp.concatenate([weight[:EDGE]] * 2, axis=1) for weight in weights]
+        bottoms = [jnp.concatenate([weight[128 - EDGE :]] * 2, axis=1) for weight in weights]
         for tile in range(samples // TILE):
             cols = slice(tile * TILE, (tile + 1) * TILE)
             [noise] = noise_tiles(tp, m, dips, rows, (tile,))
@@ -224,10 +232,8 @@
                 keep = g * per + i < count[0]
                 top = noise[i * 32 : i * 32 + 16]
                 bottom = noise[i * 32 + 16 : i * 32 + 32]
-                wt = jnp.concatenate([w[i, :EDGE]] * 2, axis=1)
-                wb = jnp.concatenate([w[i, 128 - EDGE :]] * 2, axis=1)
-                top = xt[i, :EDGE, cols].astype(F32) - wt * top
-                bottom = xb[i, EDGE:, cols].astype(F32) - wb * bottom
+                top = xt[i, :EDGE, cols].astype(F32) - tops[i] * top
+                bottom = xb[i, EDGE:, cols].astype(F32) - bottoms[i] * bottom
                 res[g, i, :EDGE, cols] = jnp.where(keep, top, 0.0).astype(BF16)
                 res[g, i, EDGE:, cols] = jnp.where(keep, bottom, 0.0).astype(BF16)
         for copy in copies(g):
@@ -258,7 +264,7 @@
                 pl.BlockSpec((per, 32, samples), lambda g, n: (last(g, n), 0, 0)),
                 pl.BlockSpec((per, 32, samples), lambda g, n: (last(g, n), 3, 0)),
                 pl.BlockSpec((halo.shape[0], per * 32, 128), lambda g, n: (0, last(g, n), 0)),
-                pl.BlockSpec((per, block, 128), lambda g, n: (last(g, n), 0, 0)),
+                pl.BlockSpec((per, 1, block), lambda g, n: (last(g, n), 0, 0)),
                 pl.BlockSpec(taps_x.shape, lambda g, n: (0, 0)),
                 pl.BlockSpec(taps_t.shape, lambda g, n: (0, 0)),
                 pl.BlockSpec(memory_space=pl.ANY),
@@ -293,7 +299,7 @@
         o[s, slots * 32 :, 0:slots] = place
 
 
-def payload(block_count, slot_dest, slot_offset, x, steps=4):
+def payload(block_count, slot_dest, slot_offset, x, steps=2):
     slots, block, samples = x.shape
     slices = samples // 128
     per = slices // steps
@@ -382,16 +388,14 @@
 
     amps = lax.all_gather(amp_table, "shot", axis=0, tiled=True)
     table_hit = amp_index[0][:, :, None] == jnp.arange(amps.shape[0], dtype=jnp.int32)
-    weight = jnp.sum(jnp.where(table_hit, amps, F32(0.0)), axis=2)
-    weight = jnp.broadcast_to(weight[:, :, None], (slots, block, 128))
-    taps_x, taps_t = spread_taps(dip_trace, dip_time)
-
-    out = interior(count, x, weight, taps_x, taps_t, 0, FIRST)
+    weight = jnp.sum(jnp.where(table_hit, amps, F32(0.0)), axis=2)[:, None]
+
+    out = interior(count, x, weight, dip_trace, dip_time, 0, FIRST)
     ends, out = lax.optimization_barrier((ends, out))
     moved = permute(ends, slots)
     halo = lax.all_to_all(moved, "rline", split_axis=0, concat_axis=0, tiled=True)
-    out = interior(count, x, weight, taps_x, taps_t, FIRST, slots - FIRST, out)
-    out = edges(count, x, halo, weight, taps_x, taps_t, out)
+    out = interior(count, x, weight, dip_trace, dip_time, FIRST, slots - FIRST, out)
+    out = edges(count, x, halo, weight, dip_trace, dip_time, out)
     return out[None]
 
 

time: 104 us -> 104 us (level)
  the two profiles are of different devices: /device:TPU:0 before, /device:TPU:32 now
where the time goes in v6:
time: 104 us; the launch traced here: 103 us
  Pallas kernels  57.8 us (56%)
  waiting for transfers between devices  16.6 us (16%)
  starting transfers between devices  13.9 us (13%)
  blocking collectives  10.5 us (10%)
  local copies, waits for them, and re-layouts  2.03 us (2%)
  other arithmetic  1.44 us (1%)
    pallas_call x2, Pallas kernels, interior(): pl.pallas_call(functools.partial(interior_kernel, start), out_shape=jax.S...  36.3 us
    all_to_all x1, waiting for transfers between devices, shards(): lax.all_to_all(moved, 'rline', split_axis=0, concat_axis=0, tiled=True)  15.5 us
    pallas_call x1, Pallas kernels, edges(): pl.pallas_call(functools.partial(edge_kernel, groups), out_shape=jax.Shap...  15.3 us
    all_gather x1, blocking collectives, shards(): amps = lax.all_gather(amp_table, 'shot', axis=0, tiled=True)  10.5 us
    all_to_all x1, starting transfers between devices, shards(): lax.all_to_all(ends, 'rline', split_axis=0, concat_axis=0, tiled=True)  8.06 us
    all_to_all x1, starting transfers between devices, shards(): lax.all_to_all(moved, 'rline', split_axis=0, concat_axis=0, tiled=True)  5.82 us
    pallas_call x1, Pallas kernels, permute(): pl.pallas_call(functools.partial(permute_kernel, slots), out_shape=jax.Sh...  3.32 us
    pallas_call x1, Pallas kernels, payload(): pl.pallas_call(functools.partial(payload_kernel, slots // 2), out_shape=j...  2.94 us
  transfers between devices with their start and end apart: 2, of which 2 were waited for; matrix products, arithmetic and copies ran while one was open for 2% of the time, Pallas kernels for 35%

profile of v6, /device:TPU:32, one launch (start us, length us, event | category | flops | bytes accessed | tf_op | source)
XLA Modules:
  0.0 103.0 jit_solution(110637458076000087)
XLA Ops:
  0.7 0.0 copy-start.4
  0.7 0.0 copy-start.5
  0.7 2.9 %payload.1 = bf16[16,592,128]{2,1,0:T(8,128)(2,1)} custom-call(s32[1,1]{1,0:T(1,128)} %copy.16.count, s32[1,18]{1,0:T(1,128)} %dest.1, s32[1,18]{1,0:T(1,128)} %offset.1, bf16[18,128,2048]{2,1,0:T(8,128)(2,1)} %bitcast.13, bf16[18,128,2048]{2,1,0:T(8,128)(2,1)} %bitcast.14), custom_call_target="tpu_custom_call" | custom-call | bytes 4194304 | tf_op jit(solution)/shard_map/payload/pallas_call | solution.py:306
  3.6 8.1 %all-to-all-start = ((bf16[16,592,128]{2,1,0:T(8,128)(2,1)}), bf16[16,592,128]{2,1,0:T(8,128)(2,1)S(1)}, u32[]{:S(2)}, u32[]{:S(2)}) async-start(bf16[16,592,128]{2,1,0:T(8,128)(2,1)} %payload.1), calls=%async_computation | async-start | bytes 4849664 | tf_op jit(solution)/shard_map/all_to_all | solution.py:387
  11.7 0.0 copy-done.4
  11.7 0.0 copy-done.5
  11.7 10.5 %all-gather = f32[8,1,128]{2,1,0:T(1,128)S(1)} all-gather(f32[1,1,128]{2,1,0:T(1,128)S(1)} %bitcast.21), channel_id=1, replica_groups=mesh['shot'=8,'rline'=16] {'shot'}, dimensions={0}, use_global_device_ids=true | all-gather | bytes 4608 | tf_op jit(solution)/shard_map/all_gather | solution.py:389
  22.2 1.4 %select_reduce_fusion = f32[18,128]{1,0:T(8,128)S(1)} fusion(f32[1024]{0:T(1024)S(1)} %bitcast.20, s32[18,128]{1,0:T(8,128)S(1)} %bitcast.19), kind=kLoop, calls=%fused_computation | loop fusion | flops 7075584 | bytes 22528 | tf_op jit(solution)/shard_map/reduce_sum | solution.py:391
  23.6 0.6 broadcast_in_dim.17.w
  24.2 19.4 %interior.2.refs_0_ = bf16[18,128,2048]{2,1,0:T(8,128)(2,1)} custom-call(s32[1]{0:T(128)} %bitcast.9.count, bf16[18,128,2048]{2,1,0:T(8,128)(2,1)} %bitcast.15, f32[18,1,128]{2,1,0:T(1,128)} %broadcast_in_dim.17.w, bf16[8,32]{1,0:T(8,128)(2,1)} %taps_x.5, bf16[8,64]{1,0:T(8,128)(2,1)} %taps_t.5), custom_call_target="tpu_custom_call" | custom-call | flops 16000000000 | bytes 8388608 | tf_op jit(solution)/shard_map/interior/pallas_call | solution.py:149
  43.7 1.1 %all-to-all-done = bf16[16,592,128]{2,1,0:T(8,128)(2,1)S(1)} async-done(((bf16[16,592,128]{2,1,0:T(8,128)(2,1)}), bf16[16,592,128]{2,1,0:T(8,128)(2,1)S(1)}, u32[]{:S(2)}, u32[]{:S(2)}) %all-to-all-start) | async-done | bytes 2424864 | tf_op jit(solution)/shard_map/all_to_all | solution.py:387
  44.8 3.3 %permute.1 = bf16[16,576,128]{2,1,0:T(8,128)(2,1)S(1)} custom-call(bf16[9472,128]{1,0:T(8,128)(2,1)S(1)} %bitcast.12), custom_call_target="tpu_custom_call" | custom-call | bytes 8388608 | tf_op jit(solution)/shard_map/permute/pallas_call | solution.py:362
  48.1 0.0 copy-start
  48.2 1.4 %copy-done = bf16[16,576,128]{2,1,0:T(8,128)(2,1)} copy-done((bf16[16,576,128]{2,1,0:T(8,128)(2,1)}, bf16[16,576,128]{2,1,0:T(8,128)(2,1)S(1)}, u32[]{:S(2)}) %copy-start) | copy-done | bytes 2359320
  49.6 5.8 %all-to-all-start.1 = ((bf16[16,576,128]{2,1,0:T(8,128)(2,1)}), bf16[16,576,128]{2,1,0:T(8,128)(2,1)S(1)}, u32[]{:S(2)}, u32[]{:S(2)}) async-start(bf16[16,576,128]{2,1,0:T(8,128)(2,1)} %copy-done), calls=%async_computation.1 | async-start | bytes 4718592 | tf_op jit(solution)/shard_map/all_to_all | solution.py:396
  55.4 0.0 copy-start.1
  55.4 0.0 copy-start.2
  55.4 0.0 copy-start.3
  55.4 16.8 %interior.3._ = bf16[18,128,2048]{2,1,0:T(8,128)(2,1)} custom-call(s32[1]{0:T(128)} %bitcast.10.count, bf16[18,128,2048]{2,1,0:T(8,128)(2,1)} %bitcast.16, f32[18,1,128]{2,1,0:T(1,128)} %broadcast_in_dim.17.w, bf16[8,32]{1,0:T(8,128)(2,1)} %taps_x.5, bf16[8,64]{1,0:T(8,128)(2,1)} %taps_t.5, ...), custom_call_target="tpu_custom_call", output_to_operand_aliasing={{}: (5, {})} | custom-call | flops 20000000000 | bytes 10485760 | tf_op jit(solution)/shard_map/interior/pallas_call | solution.py:149
  72.2 15.5 %all-to-all-done.1.halo = bf16[16,576,128]{2,1,0:T(8,128)(2,1)S(1)} async-done(((bf16[16,576,128]{2,1,0:T(8,128)(2,1)}), bf16[16,576,128]{2,1,0:T(8,128)(2,1)S(1)}, u32[]{:S(2)}, u32[]{:S(2)}) %all-to-all-start.1) | async-done | bytes 2359328 | tf_op jit(solution)/shard_map/all_to_all | solution.py:396
  87.7 0.0 copy-done.1
  87.7 0.0 copy-done.2
  87.7 0.0 copy-done.3
  87.7 15.3 %edges.1 = bf16[18,128,2048]{2,1,0:T(8,128)(2,1)} custom-call(s32[1]{0:T(128)} %bitcast.11.count, bf16[18,128,2048]{2,1,0:T(8,128)(2,1)} %bitcast.17, bf16[18,128,2048]{2,1,0:T(8,128)(2,1)} %bitcast.18, bf16[16,576,128]{2,1,0:T(8,128)(2,1)S(1)} %all-to-all-done.1.halo, f32[18,1,128]{2,1,0:T(1,128)S(1)} %copy-done.1, ...), custom_call_target="tpu_custom_call", output_to_operand_aliasing={{}: (7, {})} | custom-call | flops 8000000000 | bytes 8388608 | tf_op jit(solution)/shard_map/edges/pallas_call | solution.py:257
  (1 shorter events, 0.0 us)
Async XLA Ops:
  0.7 11.0 %copy-start.4 = (s32[1,18,128]{2,0,1:T(1,128)S(1)}, s32[1,18,128]{2,0,1:T(1,128)}, u32[]{:S(2)}) copy-start(s32[1,18,128]{2,0,1:T(1,128)} %param.12) | copy-start | bytes 27652
  0.7 11.0 %copy-start.5 = (f32[128]{0:T(128)S(1)}, f32[128]{0:T(128)}, u32[]{:S(2)}) copy-start(f32[128]{0:T(128)} %param.13) | copy-start | bytes 1540
  3.6 41.2 %all-to-all-start = ((bf16[16,592,128]{2,1,0:T(8,128)(2,1)}), bf16[16,592,128]{2,1,0:T(8,128)(2,1)S(1)}, u32[]{:S(2)}, u32[]{:S(2)}) async-start(bf16[16,592,128]{2,1,0:T(8,128)(2,1)} %payload.1), calls=%async_computation | async-start | bytes 4849664 | tf_op jit(solution)/shard_map/all_to_all | solution.py:387
  48.1 1.4 %copy-start = (bf16[16,576,128]{2,1,0:T(8,128)(2,1)}, bf16[16,576,128]{2,1,0:T(8,128)(2,1)S(1)}, u32[]{:S(2)}) copy-start(bf16[16,576,128]{2,1,0:T(8,128)(2,1)S(1)} %permute.1) | copy-start | bytes 7077892
  49.6 38.1 %all-to-all-start.1 = ((bf16[16,576,128]{2,1,0:T(8,128)(2,1)}), bf16[16,576,128]{2,1,0:T(8,128)(2,1)S(1)}, u32[]{:S(2)}, u32[]{:S(2)}) async-start(bf16[16,576,128]{2,1,0:T(8,128)(2,1)} %copy-done), calls=%async_computation.1 | async-start | bytes 4718592 | tf_op jit(solution)/shard_map/all_to_all | solution.py:396
  55.4 32.3 %copy-start.1 = (f32[18,1,128]{2,1,0:T(1,128)S(1)}, f32[18,1,128]{2,1,0:T(1,128)}, u32[]{:S(2)}) copy-start(f32[18,1,128]{2,1,0:T(1,128)} %broadcast_in_dim.17.w) | copy-start | bytes 27652
  55.4 32.3 %copy-start.2 = (bf16[8,32]{1,0:T(8,128)(2,1)S(1)}, bf16[8,32]{1,0:T(8,128)(2,1)}, u32[]{:S(2)}) copy-start(bf16[8,32]{1,0:T(8,128)(2,1)} %taps_x.5) | copy-start | bytes 1540
  55.4 32.3 %copy-start.3 = (bf16[8,64]{1,0:T(8,128)(2,1)S(1)}, bf16[8,64]{1,0:T(8,128)(2,1)}, u32[]{:S(2)}) copy-start(bf16[8,64]{1,0:T(8,128)(2,1)} %taps_t.5) | copy-start | bytes 3076

commit v7 on v6

--- a/solution.py
+++ b/solution.py
@@ -15,7 +15,7 @@
 PAIR_K = 640
 VMEM_LIMIT = 56 * 2**20
 EDGE_VMEM = 50 * 2**20
-FIRST = 8
+FIRST = 7
 
 
 def params(limit=VMEM_LIMIT):
@@ -169,12 +169,12 @@
 
 
 def edge_kernel(
-    groups, count, xt, xb, halo, w, taps_x, taps_t, _, o, shifted, tp, res, xe, m, sems
+    groups, count, x, halo, w, taps_x, taps_t, _, o, shifted, tp, res, xe, m, own, sems, own_sems
 ):
     dips = taps_x.shape[0]
     g = pl.program_id(0)
-    per = xt.shape[0]
-    samples = xt.shape[2]
+    per = x.shape[0] // groups
+    block, samples = x.shape[1:]
     rows = per * 2 * EDGE
     n_slices = halo.shape[0]
     half = xe.shape[0] // 2
@@ -193,8 +193,24 @@
             ),
         )
 
+    def loads(group):
+        slots = pl.ds(group * per, per)
+        return [
+            pltpu.make_async_copy(
+                x.at[slots, pl.ds(k * (block - 32), 32)], own.at[k, slots], own_sems.at[group, k]
+            )
+            for k in range(2)
+        ]
+
     @pl.when(g == 0)
     def _():
+        for group in range(groups):
+
+            @pl.when(group * per < count[0])
+            def _():
+                for load in loads(group):
+                    load.start()
+
         fill_time_bands(taps_t, m)
         for i, band in enumerate(trace_bands(taps_x, 64)):
             xe[i * 32 : i * 32 + 16] = band[:16, :96]
@@ -202,6 +218,10 @@
 
     @pl.when(live)
     def _():
+        for load in loads(g):
+            load.wait()
+        xt = own.at[0, pl.ds(g * per, per)]
+        xb = own.at[1, pl.ds(g * per, per)]
         for i in range(per):
             above = [halo[s, i * 32 : i * 32 + EDGE] for s in range(n_slices)]
             below = [halo[s, i * 32 + EDGE : i * 32 + 32] for s in range(n_slices)]
@@ -261,8 +281,7 @@
             num_scalar_prefetch=1,
             grid=(groups,),
             in_specs=[
-                pl.BlockSpec((per, 32, samples), lambda g, n: (last(g, n), 0, 0)),
-                pl.BlockSpec((per, 32, samples), lambda g, n: (last(g, n), 3, 0)),
+                pl.BlockSpec(memory_space=pl.ANY),
                 pl.BlockSpec((halo.shape[0], per * 32, 128), lambda g, n: (0, last(g, n), 0)),
                 pl.BlockSpec((per, 1, block), lambda g, n: (last(g, n), 0, 0)),
                 pl.BlockSpec(taps_x.shape, lambda g, n: (0, 0)),
@@ -276,27 +295,31 @@
                 pltpu.VMEM((groups, per, 32, samples), BF16),
                 pltpu.VMEM((dips * 32, 96), BF16),
                 pltpu.VMEM((dips * PAIR_K // 2, TILE), BF16),
+                pltpu.VMEM((2, slots, 32, samples), BF16),
+                pltpu.SemaphoreType.DMA((groups, 2)),
                 pltpu.SemaphoreType.DMA((groups, 2)),
             ],
         ),
-        input_output_aliases={7: 0},
+        input_output_aliases={6: 0},
         compiler_params=params(EDGE_VMEM),
         cost_estimate=cost(8_000_000_000, 2**23),
         name="edges",
-    )(count, x, x, halo, w, taps_x, taps_t, out)
+    )(count, x, halo, w, taps_x, taps_t, out)
 
 
 def payload_kernel(per_line, count, dest, offset, xt, xb, o):
     slots = xt.shape[0]
     slot = lax.broadcasted_iota(jnp.int32, (1, slots), 1)
-    place = jnp.where(slot < count[0, 0], dest[...] * per_line + offset[...], -2)
-    place = jnp.broadcast_to(place.astype(F32), (EDGE, slots)).astype(BF16)
+    place = jnp.where(slot < count[0, 0], dest[...] * per_line + offset[...], -2).astype(F32)
+    place = jnp.concatenate([place, jnp.zeros((1, 128 - slots), F32)], axis=1)
+    place = jnp.broadcast_to(place, (EDGE, 128)).astype(BF16)
+    row = lax.broadcasted_iota(jnp.int32, (EDGE, 128), 0)
     for s in range(o.shape[0]):
         cols = slice(s * 128, (s + 1) * 128)
         for i in range(slots):
-            o[s, i * 32 : i * 32 + EDGE] = xt[i, :, cols]
+            top = xt[i, :, cols]
+            o[s, i * 32 : i * 32 + EDGE] = jnp.where(row < EDGE - 1, top, place) if i == 0 else top
             o[s, i * 32 + EDGE : i * 32 + 32] = xb[i, :, cols]
-        o[s, slots * 32 :, 0:slots] = place
 
 
 def payload(block_count, slot_dest, slot_offset, x, steps=2):
@@ -305,7 +328,7 @@
     per = slices // steps
     return pl.pallas_call(
         functools.partial(payload_kernel, slots // 2),
-        out_shape=jax.ShapeDtypeStruct((slices, slots * 32 + EDGE, 128), BF16),
+        out_shape=jax.ShapeDtypeStruct((slices, slots * 32, 128), BF16),
         grid=(steps,),
         in_specs=[
             pl.BlockSpec(memory_space=pltpu.SMEM),
@@ -314,7 +337,7 @@
             pl.BlockSpec((slots, EDGE, per * 128), lambda i: (0, 0, i)),
             pl.BlockSpec((slots, EDGE, per * 128), lambda i: (0, block // EDGE - 1, i)),
         ],
-        out_specs=pl.BlockSpec((per, slots * 32 + EDGE, 128), lambda i: (i, 0, 0)),
+        out_specs=pl.BlockSpec((per, slots * 32, 128), lambda i: (i, 0, 0)),
         compiler_params=params(),
         cost_estimate=cost(0, 2**22),
         name="payload",
@@ -323,10 +346,10 @@
 
 def permute_kernel(slots, x, o, places, table, where, sem):
     sources = places.shape[0]
-    stride = slots * 32 + EDGE
+    stride = slots * 32
     for s in range(sources):
-        row = x[s * stride + slots * 32 : (s + 1) * stride]
-        places[s : s + 1] = row.astype(F32)[:1].astype(jnp.int32)
+        rows = x[s * stride : s * stride + EDGE].astype(F32)
+        places[s : s + 1] = rows[EDGE - 1 :].astype(jnp.int32)
     copy = pltpu.make_async_copy(places, table, sem)
     copy.start()
     copy.wait()

time: 104 us -> 103 us (level)
  the two profiles are of different devices: /device:TPU:32 before, /device:TPU:0 now
where the time goes in v7:
time: 103 us
  Pallas kernels  64.8 us (63%)
  starting transfers between devices  11.9 us (12%)
  waiting for transfers between devices  11.7 us (11%)
  blocking collectives  10.5 us (10%)
  local copies, waits for them, and re-layouts  2.03 us (2%)
  other arithmetic  1.44 us (1%)
    pallas_call x2, Pallas kernels, interior(): pl.pallas_call(functools.partial(interior_kernel, start), out_shape=jax.S...  43.2 us
    pallas_call x1, Pallas kernels, edges(): pl.pallas_call(functools.partial(edge_kernel, groups), out_shape=jax.Shap...  15.3 us
    all_gather x1, blocking collectives, shards(): amps = lax.all_gather(amp_table, 'shot', axis=0, tiled=True)  10.5 us
    all_to_all x1, starting transfers between devices, shards(): lax.all_to_all(ends, 'rline', split_axis=0, concat_axis=0, tiled=True)  8.13 us
    all_to_all x1, waiting for transfers between devices, shards(): lax.all_to_all(moved, 'rline', split_axis=0, concat_axis=0, tiled=True)  7.94 us
    all_to_all x1, waiting for transfers between devices, shards(): lax.all_to_all(ends, 'rline', split_axis=0, concat_axis=0, tiled=True)  3.79 us
    all_to_all x1, starting transfers between devices, shards(): lax.all_to_all(moved, 'rline', split_axis=0, concat_axis=0, tiled=True)  3.72 us
    pallas_call x1, Pallas kernels, permute(): pl.pallas_call(functools.partial(permute_kernel, slots), out_shape=jax.Sh...  3.32 us
  transfers between devices with their start and end apart: 2, of which 2 were waited for; matrix products, arithmetic and copies ran while one was open for 2% of the time, Pallas kernels for 42%

profile of v7, /device:TPU:0, one launch (start us, length us, event | category | flops | bytes accessed | tf_op | source)
XLA Modules:
  0.0 103.1 jit_solution(14989839747229810320)
XLA Ops:
  0.7 0.0 copy-start.4
  0.7 0.0 copy-start.5
  0.7 2.9 %payload.1 = bf16[16,576,128]{2,1,0:T(8,128)(2,1)} custom-call(s32[1,1]{1,0:T(1,128)} %copy.16.count, s32[1,18]{1,0:T(1,128)} %dest.1, s32[1,18]{1,0:T(1,128)} %offset.1, bf16[18,128,2048]{2,1,0:T(8,128)(2,1)} %bitcast.13, bf16[18,128,2048]{2,1,0:T(8,128)(2,1)} %bitcast.14), custom_call_target="tpu_custom_call" | custom-call | bytes 4194304 | tf_op jit(solution)/shard_map/payload/pallas_call | solution.py:329
  3.6 8.1 %all-to-all-start = ((bf16[16,576,128]{2,1,0:T(8,128)(2,1)}), bf16[16,576,128]{2,1,0:T(8,128)(2,1)S(1)}, u32[]{:S(2)}, u32[]{:S(2)}) async-start(bf16[16,576,128]{2,1,0:T(8,128)(2,1)} %payload.1), calls=%async_computation | async-start | bytes 4718592 | tf_op jit(solution)/shard_map/all_to_all | solution.py:410
  11.7 0.0 copy-done.4
  11.8 0.0 copy-done.5
  11.8 10.5 %all-gather = f32[8,1,128]{2,1,0:T(1,128)S(1)} all-gather(f32[1,1,128]{2,1,0:T(1,128)S(1)} %bitcast.20), channel_id=1, replica_groups=mesh['shot'=8,'rline'=16] {'shot'}, dimensions={0}, use_global_device_ids=true | all-gather | bytes 4608 | tf_op jit(solution)/shard_map/all_gather | solution.py:412
  22.3 1.4 %select_reduce_fusion = f32[18,128]{1,0:T(8,128)S(1)} fusion(f32[1024]{0:T(1024)S(1)} %bitcast.19, s32[18,128]{1,0:T(8,128)S(1)} %bitcast.18), kind=kLoop, calls=%fused_computation | loop fusion | flops 7075584 | bytes 22528 | tf_op jit(solution)/shard_map/reduce_sum | solution.py:414
  23.7 0.6 broadcast_in_dim.17.w
  24.3 17.3 %interior.2.refs_0_ = bf16[18,128,2048]{2,1,0:T(8,128)(2,1)} custom-call(s32[1]{0:T(128)} %bitcast.9.count, bf16[18,128,2048]{2,1,0:T(8,128)(2,1)} %bitcast.15, f32[18,1,128]{2,1,0:T(1,128)} %broadcast_in_dim.17.w, bf16[8,32]{1,0:T(8,128)(2,1)} %taps_x.5, bf16[8,64]{1,0:T(8,128)(2,1)} %taps_t.5), custom_call_target="tpu_custom_call" | custom-call | flops 14000000000 | bytes 7340032 | tf_op jit(solution)/shard_map/interior/pallas_call | solution.py:149
  41.6 3.8 %all-to-all-done = bf16[16,576,128]{2,1,0:T(8,128)(2,1)S(1)} async-done(((bf16[16,576,128]{2,1,0:T(8,128)(2,1)}), bf16[16,576,128]{2,1,0:T(8,128)(2,1)S(1)}, u32[]{:S(2)}, u32[]{:S(2)}) %all-to-all-start) | async-done | bytes 2359328 | tf_op jit(solution)/shard_map/all_to_all | solution.py:410
  45.4 3.3 %permute.1 = bf16[16,576,128]{2,1,0:T(8,128)(2,1)S(1)} custom-call(bf16[9216,128]{1,0:T(8,128)(2,1)S(1)} %bitcast.12), custom_call_target="tpu_custom_call" | custom-call | bytes 8388608 | tf_op jit(solution)/shard_map/permute/pallas_call | solution.py:385
  48.7 0.0 copy-start
  48.7 1.4 %copy-done = bf16[16,576,128]{2,1,0:T(8,128)(2,1)} copy-done((bf16[16,576,128]{2,1,0:T(8,128)(2,1)}, bf16[16,576,128]{2,1,0:T(8,128)(2,1)S(1)}, u32[]{:S(2)}) %copy-start) | copy-done | bytes 2359320
  50.1 3.7 %all-to-all-start.1 = ((bf16[16,576,128]{2,1,0:T(8,128)(2,1)}), bf16[16,576,128]{2,1,0:T(8,128)(2,1)S(1)}, u32[]{:S(2)}, u32[]{:S(2)}) async-start(bf16[16,576,128]{2,1,0:T(8,128)(2,1)} %copy-done), calls=%async_computation.1 | async-start | bytes 4718592 | tf_op jit(solution)/shard_map/all_to_all | solution.py:419
  53.9 0.0 copy-start.1
  53.9 0.0 copy-start.2
  53.9 0.0 copy-start.3
  53.9 25.9 %interior.3._ = bf16[18,128,2048]{2,1,0:T(8,128)(2,1)} custom-call(s32[1]{0:T(128)} %bitcast.10.count, bf16[18,128,2048]{2,1,0:T(8,128)(2,1)} %bitcast.16, f32[18,1,128]{2,1,0:T(1,128)} %broadcast_in_dim.17.w, bf16[8,32]{1,0:T(8,128)(2,1)} %taps_x.5, bf16[8,64]{1,0:T(8,128)(2,1)} %taps_t.5, ...), custom_call_target="tpu_custom_call", output_to_operand_aliasing={{}: (5, {})} | custom-call | flops 22000001024 | bytes 11534336 | tf_op jit(solution)/shard_map/interior/pallas_call | solution.py:149
  79.8 7.9 %all-to-all-done.1.halo = bf16[16,576,128]{2,1,0:T(8,128)(2,1)S(1)} async-done(((bf16[16,576,128]{2,1,0:T(8,128)(2,1)}), bf16[16,576,128]{2,1,0:T(8,128)(2,1)S(1)}, u32[]{:S(2)}, u32[]{:S(2)}) %all-to-all-start.1) | async-done | bytes 2359328 | tf_op jit(solution)/shard_map/all_to_all | solution.py:419
  87.8 0.0 copy-done.1
  87.8 0.0 copy-done.2
  87.8 0.0 copy-done.3
  87.8 15.3 %edges.1 = bf16[18,128,2048]{2,1,0:T(8,128)(2,1)} custom-call(s32[1]{0:T(128)} %bitcast.11.count, bf16[18,128,2048]{2,1,0:T(8,128)(2,1)} %bitcast.17, bf16[16,576,128]{2,1,0:T(8,128)(2,1)S(1)} %all-to-all-done.1.halo, f32[18,1,128]{2,1,0:T(1,128)S(1)} %copy-done.1, bf16[8,32]{1,0:T(8,128)(2,1)S(1)} %copy-done.2, ...), custom_call_target="tpu_custom_call", output_to_operand_aliasing={{}: (6, {})} | custom-call | flops 8000000000 | bytes 8388608 | tf_op jit(solution)/shard_map/edges/pallas_call | solution.py:277
  (1 shorter events, 0.0 us)
Async XLA Ops:
  0.7 11.1 %copy-start.4 = (s32[1,18,128]{2,0,1:T(1,128)S(1)}, s32[1,18,128]{2,0,1:T(1,128)}, u32[]{:S(2)}) copy-start(s32[1,18,128]{2,0,1:T(1,128)} %param.12) | copy-start | bytes 27652
  0.7 11.1 %copy-start.5 = (f32[128]{0:T(128)S(1)}, f32[128]{0:T(128)}, u32[]{:S(2)}) copy-start(f32[128]{0:T(128)} %param.13) | copy-start | bytes 1540
  3.6 41.8 %all-to-all-start = ((bf16[16,576,128]{2,1,0:T(8,128)(2,1)}), bf16[16,576,128]{2,1,0:T(8,128)(2,1)S(1)}, u32[]{:S(2)}, u32[]{:S(2)}) async-start(bf16[16,576,128]{2,1,0:T(8,128)(2,1)} %payload.1), calls=%async_computation | async-start | bytes 4718592 | tf_op jit(solution)/shard_map/all_to_all | solution.py:410
  48.7 1.4 %copy-start = (bf16[16,576,128]{2,1,0:T(8,128)(2,1)}, bf16[16,576,128]{2,1,0:T(8,128)(2,1)S(1)}, u32[]{:S(2)}) copy-start(bf16[16,576,128]{2,1,0:T(8,128)(2,1)S(1)} %permute.1) | copy-start | bytes 7077892
  50.1 37.7 %all-to-all-start.1 = ((bf16[16,576,128]{2,1,0:T(8,128)(2,1)}), bf16[16,576,128]{2,1,0:T(8,128)(2,1)S(1)}, u32[]{:S(2)}, u32[]{:S(2)}) async-start(bf16[16,576,128]{2,1,0:T(8,128)(2,1)} %copy-done), calls=%async_computation.1 | async-start | bytes 4718592 | tf_op jit(solution)/shard_map/all_to_all | solution.py:419
  53.9 33.9 %copy-start.1 = (f32[18,1,128]{2,1,0:T(1,128)S(1)}, f32[18,1,128]{2,1,0:T(1,128)}, u32[]{:S(2)}) copy-start(f32[18,1,128]{2,1,0:T(1,128)} %broadcast_in_dim.17.w) | copy-start | bytes 27652
  53.9 33.9 %copy-start.2 = (bf16[8,32]{1,0:T(8,128)(2,1)S(1)}, bf16[8,32]{1,0:T(8,128)(2,1)}, u32[]{:S(2)}) copy-start(bf16[8,32]{1,0:T(8,128)(2,1)} %taps_x.5) | copy-start | bytes 1540
  53.9 33.9 %copy-start.3 = (bf16[8,64]{1,0:T(8,128)(2,1)S(1)}, bf16[8,64]{1,0:T(8,128)(2,1)}, u32[]{:S(2)}) copy-start(bf16[8,64]{1,0:T(8,128)(2,1)} %taps_t.5) | copy-start | bytes 3076

commit v8 on v7

--- a/solution.py
+++ b/solution.py
@@ -15,7 +15,7 @@
 PAIR_K = 640
 VMEM_LIMIT = 56 * 2**20
 EDGE_VMEM = 50 * 2**20
-FIRST = 7
+FIRST = 6
 
 
 def params(limit=VMEM_LIMIT):
@@ -223,8 +223,9 @@
         xt = own.at[0, pl.ds(g * per, per)]
         xb = own.at[1, pl.ds(g * per, per)]
         for i in range(per):
-            above = [halo[s, i * 32 : i * 32 + EDGE] for s in range(n_slices)]
-            below = [halo[s, i * 32 + EDGE : i * 32 + 32] for s in range(n_slices)]
+            at = pl.multiple_of((g * per + i) * 32, 32)
+            above = [halo[s, pl.ds(at, EDGE)] for s in range(n_slices)]
+            below = [halo[s, pl.ds(at + EDGE, EDGE)] for s in range(n_slices)]
             above = jnp.concatenate(above, axis=1)
             below = jnp.concatenate(below, axis=1)
             for k in range(2):
@@ -282,7 +283,7 @@
             grid=(groups,),
             in_specs=[
                 pl.BlockSpec(memory_space=pl.ANY),
-                pl.BlockSpec((halo.shape[0], per * 32, 128), lambda g, n: (0, last(g, n), 0)),
+                pl.BlockSpec(memory_space=pltpu.VMEM),
                 pl.BlockSpec((per, 1, block), lambda g, n: (last(g, n), 0, 0)),
                 pl.BlockSpec(taps_x.shape, lambda g, n: (0, 0)),
                 pl.BlockSpec(taps_t.shape, lambda g, n: (0, 0)),

time: 103 us -> 99.9 us (0.970)
  the two profiles are of different devices: /device:TPU:0 before, /device:TPU:36 now
where the time goes in v8:
time: 99.9 us; the launch traced here: 98.2 us
  Pallas kernels  57.5 us (58%)
  waiting for transfers between devices  15.1 us (15%)
  starting transfers between devices  13 us (13%)
  blocking collectives  8.33 us (8%)
  local copies, waits for them, and re-layouts  2.03 us (2%)
  other arithmetic  1.44 us (1%)
    pallas_call x2, Pallas kernels, interior(): pl.pallas_call(functools.partial(interior_kernel, start), out_shape=jax.S...  36.3 us
    pallas_call x1, Pallas kernels, edges(): pl.pallas_call(functools.partial(edge_kernel, groups), out_shape=jax.Shap...  15 us
    all_gather x1, blocking collectives, shards(): amps = lax.all_gather(amp_table, 'shot', axis=0, tiled=True)  8.33 us
    all_to_all x1, waiting for transfers between devices, shards(): lax.all_to_all(moved, 'rline', split_axis=0, concat_axis=0, tiled=True)  8.33 us
    all_to_all x1, starting transfers between devices, shards(): lax.all_to_all(ends, 'rline', split_axis=0, concat_axis=0, tiled=True)  8.06 us
    all_to_all x1, waiting for transfers between devices, shards(): lax.all_to_all(ends, 'rline', split_axis=0, concat_axis=0, tiled=True)  6.75 us
    all_to_all x1, starting transfers between devices, shards(): lax.all_to_all(moved, 'rline', split_axis=0, concat_axis=0, tiled=True)  4.97 us
    pallas_call x1, Pallas kernels, permute(): pl.pallas_call(functools.partial(permute_kernel, slots), out_shape=jax.Sh...  3.32 us
  transfers between devices with their start and end apart: 2, of which 2 were waited for; matrix products, arithmetic and copies ran while one was open for 2% of the time, Pallas kernels for 37%

profile of v8, /device:TPU:36, one launch (start us, length us, event | category | flops | bytes accessed | tf_op | source)
XLA Modules:
  0.0 98.2 jit_solution(4704620538140046174)
XLA Ops:
  0.7 0.0 copy-start.4
  0.7 0.0 copy-start.5
  0.7 2.9 %payload.1 = bf16[16,576,128]{2,1,0:T(8,128)(2,1)} custom-call(s32[1,1]{1,0:T(1,128)} %copy.16.count, s32[1,18]{1,0:T(1,128)} %dest.1, s32[1,18]{1,0:T(1,128)} %offset.1, bf16[18,128,2048]{2,1,0:T(8,128)(2,1)} %bitcast.13, bf16[18,128,2048]{2,1,0:T(8,128)(2,1)} %bitcast.14), custom_call_target="tpu_custom_call" | custom-call | bytes 4194304 | tf_op jit(solution)/shard_map/payload/pallas_call | solution.py:330
  3.6 8.1 %all-to-all-start = ((bf16[16,576,128]{2,1,0:T(8,128)(2,1)}), bf16[16,576,128]{2,1,0:T(8,128)(2,1)S(1)}, u32[]{:S(2)}, u32[]{:S(2)}) async-start(bf16[16,576,128]{2,1,0:T(8,128)(2,1)} %payload.1), calls=%async_computation | async-start | bytes 4718592 | tf_op jit(solution)/shard_map/all_to_all | solution.py:411
  11.7 0.0 copy-done.4
  11.7 0.0 copy-done.5
  11.7 8.3 %all-gather = f32[8,1,128]{2,1,0:T(1,128)S(1)} all-gather(f32[1,1,128]{2,1,0:T(1,128)S(1)} %bitcast.20), channel_id=1, replica_groups=mesh['shot'=8,'rline'=16] {'shot'}, dimensions={0}, use_global_device_ids=true | all-gather | bytes 4608 | tf_op jit(solution)/shard_map/all_gather | solution.py:413
  20.0 1.4 %select_reduce_fusion = f32[18,128]{1,0:T(8,128)S(1)} fusion(f32[1024]{0:T(1024)S(1)} %bitcast.19, s32[18,128]{1,0:T(8,128)S(1)} %bitcast.18), kind=kLoop, calls=%fused_computation | loop fusion | flops 7075584 | bytes 22528 | tf_op jit(solution)/shard_map/reduce_sum | solution.py:415
  21.5 0.6 broadcast_in_dim.17.w
  22.1 15.2 %interior.2.refs_0_ = bf16[18,128,2048]{2,1,0:T(8,128)(2,1)} custom-call(s32[1]{0:T(128)} %bitcast.9.count, bf16[18,128,2048]{2,1,0:T(8,128)(2,1)} %bitcast.15, f32[18,1,128]{2,1,0:T(1,128)} %broadcast_in_dim.17.w, bf16[8,32]{1,0:T(8,128)(2,1)} %taps_x.5, bf16[8,64]{1,0:T(8,128)(2,1)} %taps_t.5), custom_call_target="tpu_custom_call" | custom-call | flops 12000000000 | bytes 6291456 | tf_op jit(solution)/shard_map/interior/pallas_call | solution.py:149
  37.2 6.7 %all-to-all-done = bf16[16,576,128]{2,1,0:T(8,128)(2,1)S(1)} async-done(((bf16[16,576,128]{2,1,0:T(8,128)(2,1)}), bf16[16,576,128]{2,1,0:T(8,128)(2,1)S(1)}, u32[]{:S(2)}, u32[]{:S(2)}) %all-to-all-start) | async-done | bytes 2359328 | tf_op jit(solution)/shard_map/all_to_all | solution.py:411
  44.0 3.3 %permute.1 = bf16[16,576,128]{2,1,0:T(8,128)(2,1)S(1)} custom-call(bf16[9216,128]{1,0:T(8,128)(2,1)S(1)} %bitcast.12), custom_call_target="tpu_custom_call" | custom-call | bytes 8388608 | tf_op jit(solution)/shard_map/permute/pallas_call | solution.py:386
  47.3 0.0 copy-start
  47.3 1.4 %copy-done = bf16[16,576,128]{2,1,0:T(8,128)(2,1)} copy-done((bf16[16,576,128]{2,1,0:T(8,128)(2,1)}, bf16[16,576,128]{2,1,0:T(8,128)(2,1)S(1)}, u32[]{:S(2)}) %copy-start) | copy-done | bytes 2359320
  48.7 5.0 %all-to-all-start.1 = ((bf16[16,576,128]{2,1,0:T(8,128)(2,1)}), bf16[16,576,128]{2,1,0:T(8,128)(2,1)S(1)}, u32[]{:S(2)}, u32[]{:S(2)}) async-start(bf16[16,576,128]{2,1,0:T(8,128)(2,1)} %copy-done), calls=%async_computation.1 | async-start | bytes 4718592 | tf_op jit(solution)/shard_map/all_to_all | solution.py:420
  53.7 0.0 copy-start.1
  53.7 0.0 copy-start.2
  53.7 0.0 copy-start.3
  53.7 21.1 %interior.3._ = bf16[18,128,2048]{2,1,0:T(8,128)(2,1)} custom-call(s32[1]{0:T(128)} %bitcast.10.count, bf16[18,128,2048]{2,1,0:T(8,128)(2,1)} %bitcast.16, f32[18,1,128]{2,1,0:T(1,128)} %broadcast_in_dim.17.w, bf16[8,32]{1,0:T(8,128)(2,1)} %taps_x.5, bf16[8,64]{1,0:T(8,128)(2,1)} %taps_t.5, ...), custom_call_target="tpu_custom_call", output_to_operand_aliasing={{}: (5, {})} | custom-call | flops 24000000000 | bytes 12582912 | tf_op jit(solution)/shard_map/interior/pallas_call | solution.py:149
  74.8 8.3 %all-to-all-done.1.halo = bf16[16,576,128]{2,1,0:T(8,128)(2,1)S(1)} async-done(((bf16[16,576,128]{2,1,0:T(8,128)(2,1)}), bf16[16,576,128]{2,1,0:T(8,128)(2,1)S(1)}, u32[]{:S(2)}, u32[]{:S(2)}) %all-to-all-start.1) | async-done | bytes 2359328 | tf_op jit(solution)/shard_map/all_to_all | solution.py:420
  83.2 0.0 copy-done.1
  83.2 0.0 copy-done.2
  83.2 0.0 copy-done.3
  83.2 15.0 %edges.1 = bf16[18,128,2048]{2,1,0:T(8,128)(2,1)} custom-call(s32[1]{0:T(128)} %bitcast.11.count, bf16[18,128,2048]{2,1,0:T(8,128)(2,1)} %bitcast.17, bf16[16,576,128]{2,1,0:T(8,128)(2,1)S(1)} %all-to-all-done.1.halo, f32[18,1,128]{2,1,0:T(1,128)S(1)} %copy-done.1, bf16[8,32]{1,0:T(8,128)(2,1)S(1)} %copy-done.2, ...), custom_call_target="tpu_custom_call", output_to_operand_aliasing={{}: (6, {})} | custom-call | flops 8000000000 | bytes 8388608 | tf_op jit(solution)/shard_map/edges/pallas_call | solution.py:278
  (1 shorter events, 0.0 us)
Async XLA Ops:
  0.7 11.0 %copy-start.4 = (s32[1,18,128]{2,0,1:T(1,128)S(1)}, s32[1,18,128]{2,0,1:T(1,128)}, u32[]{:S(2)}) copy-start(s32[1,18,128]{2,0,1:T(1,128)} %param.12) | copy-start | bytes 27652
  0.7 11.0 %copy-start.5 = (f32[128]{0:T(128)S(1)}, f32[128]{0:T(128)}, u32[]{:S(2)}) copy-start(f32[128]{0:T(128)} %param.13) | copy-start | bytes 1540
  3.6 40.4 %all-to-all-start = ((bf16[16,576,128]{2,1,0:T(8,128)(2,1)}), bf16[16,576,128]{2,1,0:T(8,128)(2,1)S(1)}, u32[]{:S(2)}, u32[]{:S(2)}) async-start(bf16[16,576,128]{2,1,0:T(8,128)(2,1)} %payload.1), calls=%async_computation | async-start | bytes 4718592 | tf_op jit(solution)/shard_map/all_to_all | solution.py:411
  47.3 1.4 %copy-start = (bf16[16,576,128]{2,1,0:T(8,128)(2,1)}, bf16[16,576,128]{2,1,0:T(8,128)(2,1)S(1)}, u32[]{:S(2)}) copy-start(bf16[16,576,128]{2,1,0:T(8,128)(2,1)S(1)} %permute.1) | copy-start | bytes 7077892
  48.7 34.5 %all-to-all-start.1 = ((bf16[16,576,128]{2,1,0:T(8,128)(2,1)}), bf16[16,576,128]{2,1,0:T(8,128)(2,1)S(1)}, u32[]{:S(2)}, u32[]{:S(2)}) async-start(bf16[16,576,128]{2,1,0:T(8,128)(2,1)} %copy-done), calls=%async_computation.1 | async-start | bytes 4718592 | tf_op jit(solution)/shard_map/all_to_all | solution.py:420
  53.7 29.5 %copy-start.1 = (f32[18,1,128]{2,1,0:T(1,128)S(1)}, f32[18,1,128]{2,1,0:T(1,128)}, u32[]{:S(2)}) copy-start(f32[18,1,128]{2,1,0:T(1,128)} %broadcast_in_dim.17.w) | copy-start | bytes 27652
  53.7 29.5 %copy-start.2 = (bf16[8,32]{1,0:T(8,128)(2,1)S(1)}, bf16[8,32]{1,0:T(8,128)(2,1)}, u32[]{:S(2)}) copy-start(bf16[8,32]{1,0:T(8,128)(2,1)} %taps_x.5) | copy-start | bytes 1540
  53.7 29.5 %copy-start.3 = (bf16[8,64]{1,0:T(8,128)(2,1)S(1)}, bf16[8,64]{1,0:T(8,128)(2,1)}, u32[]{:S(2)}) copy-start(bf16[8,64]{1,0:T(8,128)(2,1)} %taps_t.5) | copy-start | bytes 3076
